TPU v7x, 256 devices: a whole 4x4x8 slice. The times are simulated.
256 devices in a mesh: tok: 32 (over x, z), head: 8 (over y, core).
Axes of the slice: x: 4, y: 4, z: 8, core: 2. Of those that a mesh axis runs over, the one named last changes fastest.
Arguments:
- queries: bfloat16 [32768, 4096], P(('tok', 'head')), may hold values from -32 to 32
- key_states: bfloat16 [32768, 512], P(('tok', 'head')), may hold values from -10 to 10
- value_states: bfloat16 [32768, 512], P(('tok', 'head')), may hold values from -6 to 6
- out_grad: bfloat16 [32768, 4096], P(('tok', 'head')), may hold values from -15 to 15
- sink_logits: float32 [64], P('head'), may hold values from 0 to 5
- branch_start: int32 [64], replicated, may hold values from 0 to 32640, as said below
- branch_len: int32 [64], replicated, may hold values from 128 to 384, as said below
- parent_list: int32 [64, 2], replicated, may hold values from -1 to 256, as said below
Outputs:
- attn_out: bfloat16 [32768, 4096], P(('tok', 'head'))
- query_grad: bfloat16 [32768, 4096], P(('tok', 'head'))
- key_grad: bfloat16 [32768, 512], P(('tok', 'head'))
- value_grad: bfloat16 [32768, 512], P(('tok', 'head'))
- sink_grad: float32 [64], P('head')
Inputs may be any that keep to these rules, and one draw needn't show every extreme that they name: `branch_start`: branch b lies within the tokens of index b // 2 of tok. The branches of one index follow one another in order, begin at multiples of 128 and do not intersect; tokens between them belong to no branch. `branch_len`: A multiple of 128. `parent_list`: row b is (parent branch, tail offset). The branches of index 0 of tok have parent -1 and offset 0; the parent of a branch on index d lies on index d - s for some s from 1 to min(3, d), and each s from 1 to 3 occurs. Branches 2m and 2m + 1 are siblings with equal rows. The offset is a multiple of 128 and the 128 tokens of the parent that begin there lie inside the parent.
All inputs are finite; a program needn't handle non-finite values.
Results may differ from a plain program's by a relative error of at most 0.02.
Values may be sent and summed in bfloat16 or wider, within the bound.
A program may use at most 64 MiB of HBM per device.

v0:
```python
import math

import jax
import jax.numpy as jnp
from jax import lax
from jax.sharding import PartitionSpec as P

HEAD_DIM = 64
WINDOW = 128
LAG = 3
TOK_DEV = 1024
BR_DEV = 2


def from_behind(value, axis, steps):
    count = lax.axis_size(axis)
    leading, last = (max(0, -steps), min(count, count - steps))
    return lax.ppermute(value, axis, [(source, source + steps) for source in range(leading, last)])


def product(spec, left, right):
    return jnp.einsum(spec, left, right, preferred_element_type=jnp.float32)


def attend(
    query_rows, key_own, value_own, key_prev, value_prev, grad_rows, prev_ok, alive, sink_table
):
    window_len = query_rows.shape[1]
    factor = 1.0 / math.sqrt(query_rows.shape[-1])
    offsets = jnp.arange(window_len)
    causal = offsets[None, :] <= offsets[:, None]
    behind = (offsets[None, :] > offsets[:, None])[None, None, None] & prev_ok[
        :, None, None, None, None
    ]
    own_scores = jnp.where(
        causal, product("bqkgd,bjkd->bkgqj", query_rows, key_own) * factor, -jnp.inf
    )
    prev_scores = jnp.where(
        behind, product("bqkgd,bjkd->bkgqj", query_rows, key_prev) * factor, -jnp.inf
    )
    sink_col = sink_table[None, :, :, None]
    peak = jnp.maximum(
        jnp.maximum(jnp.max(own_scores, axis=-1), jnp.max(prev_scores, axis=-1)), sink_col
    )
    own_exp = jnp.exp(own_scores - peak[..., None])
    prev_exp = jnp.exp(prev_scores - peak[..., None])
    sink_exp = jnp.exp(sink_col - peak)
    summed = jnp.sum(own_exp, axis=-1) + jnp.sum(prev_exp, axis=-1) + sink_exp
    own_prob = own_exp / summed[..., None]
    prev_prob = prev_exp / summed[..., None]
    own_half = own_prob.astype(jnp.bfloat16)
    prev_half = prev_prob.astype(jnp.bfloat16)
    blended = product("bkgqj,bjkd->bqkgd", own_half, value_own) + product(
        "bkgqj,bjkd->bqkgd", prev_half, value_prev
    )
    alive_rows = alive[:, None, None, None, None]
    attended = jnp.where(alive_rows, blended, 0.0).astype(jnp.bfloat16)
    grad_rows = jnp.where(alive_rows, grad_rows, jnp.zeros_like(grad_rows))
    row_delta = jnp.moveaxis(
        jnp.sum(grad_rows.astype(jnp.float32) * attended.astype(jnp.float32), axis=-1), 1, -1
    )
    own_slope = (
        own_prob * (product("bqkgd,bjkd->bkgqj", grad_rows, value_own) - row_delta[..., None])
    ).astype(jnp.bfloat16)
    prev_slope = (
        prev_prob * (product("bqkgd,bjkd->bkgqj", grad_rows, value_prev) - row_delta[..., None])
    ).astype(jnp.bfloat16)
    query_grad = (
        (
            product("bkgqj,bjkd->bqkgd", own_slope, key_own)
            + product("bkgqj,bjkd->bqkgd", prev_slope, key_prev)
        )
        * factor
    ).astype(jnp.bfloat16)
    key_own_grad = product("bkgqj,bqkgd->bjkd", own_slope, query_rows) * factor
    key_prev_grad = product("bkgqj,bqkgd->bjkd", prev_slope, query_rows) * factor
    value_own_grad = product("bkgqj,bqkgd->bjkd", own_half, grad_rows)
    value_prev_grad = product("bkgqj,bqkgd->bjkd", prev_half, grad_rows)
    sink_grad = -jnp.sum(sink_exp / summed * row_delta, axis=(0, 3))
    return (
        attended,
        query_grad,
        key_own_grad,
        value_own_grad,
        key_prev_grad,
        value_prev_grad,
        sink_grad,
    )


def fetch_each(payload, distance):
    return from_behind(payload, "tok", distance)


def return_each(payload, distance):
    return from_behind(payload, "tok", -distance)


def local(
    queries, key_states, value_states, out_grad, sink_logits, branch_start, branch_len, parent_list
):
    tok_count = lax.axis_size("tok")
    this_tok = lax.axis_index("tok")
    query_here, key_here, value_here, grad_here = (
        lax.all_to_all(queries, "head", split_axis=1, concat_axis=0, tiled=True),
        lax.all_to_all(key_states, "head", split_axis=1, concat_axis=0, tiled=True),
        lax.all_to_all(value_states, "head", split_axis=1, concat_axis=0, tiled=True),
        lax.all_to_all(out_grad, "head", split_axis=1, concat_axis=0, tiled=True),
    )
    blocks = TOK_DEV // WINDOW
    kv_dev = key_here.shape[1] // HEAD_DIM
    group_size = query_here.shape[1] // (kv_dev * HEAD_DIM)
    lane_count = WINDOW * kv_dev * HEAD_DIM
    branch_count = branch_start.shape[0]
    branch_ids = jnp.arange(branch_count, dtype=jnp.int32)
    parent = parent_list[:, 0]
    parent_start = jnp.sum(
        jnp.where(branch_ids[None, :] == parent[:, None], branch_start[None, :], 0), axis=1
    )
    tail_block = (parent_start + parent_list[:, 1]) // WINDOW
    tail_owner = (tail_block // blocks).reshape(tok_count, BR_DEV)
    tail_local = (tail_block % blocks).reshape(tok_count, BR_DEV)
    has_tail = (parent >= 0).reshape(tok_count, BR_DEV)
    home_index = (branch_ids // BR_DEV).reshape(tok_count, BR_DEV)
    distance_grid = jnp.where(has_tail, home_index - tail_owner, 0)
    my_valid = has_tail[this_tok]
    my_distance = distance_grid[this_tok]
    my_start = (
        lax.dynamic_slice_in_dim(branch_start, this_tok * BR_DEV, BR_DEV) - this_tok * TOK_DEV
    )
    my_end = my_start + lax.dynamic_slice_in_dim(branch_len, this_tok * BR_DEV, BR_DEV)
    block_pos = jnp.arange(blocks, dtype=jnp.int32) * WINDOW
    covers = (my_start[None, :] <= block_pos[:, None]) & (block_pos[:, None] < my_end[None, :])
    alive = jnp.any(covers, axis=1)
    opening = jnp.any(covers & (my_start[None, :] == block_pos[:, None]), axis=1)
    holder = jnp.sum(jnp.where(covers, jnp.arange(BR_DEV, dtype=jnp.int32)[None, :], 0), axis=1)
    prev_ok = alive & (jnp.logical_not(opening) | jnp.any(covers & my_valid[None, :], axis=1))
    kv_pairs = jnp.concatenate(
        [key_here.reshape(blocks, lane_count), value_here.reshape(blocks, lane_count)], axis=1
    )
    tail_pairs = jnp.zeros((BR_DEV, 2 * lane_count), jnp.bfloat16)
    for distance in range(1, LAG + 1):
        child_row = jnp.minimum(this_tok + distance, tok_count - 1)
        child_real = this_tok + distance < tok_count
        need = has_tail[child_row] & (distance_grid[child_row] == distance) & child_real
        payload = jnp.where(
            need[:, None], kv_pairs[tail_local[child_row]], jnp.zeros((), jnp.bfloat16)
        )
        arrived = fetch_each(payload, distance)
        tail_pairs = jnp.where((my_valid & (my_distance == distance))[:, None], arrived, tail_pairs)
    shifted = jnp.concatenate([jnp.zeros_like(kv_pairs[:1]), kv_pairs[:-1]], axis=0)
    prev_pairs = jnp.where(opening[:, None], tail_pairs[holder], shifted)
    prev_pairs = jnp.where(prev_ok[:, None], prev_pairs, jnp.zeros((), jnp.bfloat16))
    step_blocks = min(blocks, max(1, 512 // WINDOW))
    rounds = blocks // step_blocks
    query_blocks = query_here.reshape(rounds, step_blocks, WINDOW, kv_dev, group_size, HEAD_DIM)
    grad_blocks = grad_here.reshape(rounds, step_blocks, WINDOW, kv_dev, group_size, HEAD_DIM)
    key_blocks = key_here.reshape(rounds, step_blocks, WINDOW, kv_dev, HEAD_DIM)
    value_blocks = value_here.reshape(rounds, step_blocks, WINDOW, kv_dev, HEAD_DIM)
    prev_split = prev_pairs.reshape(rounds, step_blocks, 2, WINDOW, kv_dev, HEAD_DIM)
    sink_table = sink_logits.reshape(kv_dev, group_size)

    def attend_round(pieces):
        return attend(*pieces, sink_table)

    results = lax.map(
        attend_round,
        (
            query_blocks,
            key_blocks,
            value_blocks,
            prev_split[:, :, 0],
            prev_split[:, :, 1],
            grad_blocks,
            prev_ok.reshape(rounds, step_blocks),
            alive.reshape(rounds, step_blocks),
        ),
    )
    attended, query_grad, key_own, value_own, key_prev, value_prev, sink_parts = results
    own_grad = jnp.concatenate(
        [key_own.reshape(blocks, lane_count), value_own.reshape(blocks, lane_count)], axis=1
    )
    prev_grad = jnp.concatenate(
        [key_prev.reshape(blocks, lane_count), value_prev.reshape(blocks, lane_count)], axis=1
    )
    inside = jnp.where((alive & jnp.logical_not(opening))[:, None], prev_grad, 0.0)
    own_grad = own_grad + jnp.concatenate([inside[1:], jnp.zeros_like(inside[:1])], axis=0)
    tail_grad = jnp.where(my_valid[:, None], prev_grad[my_start // WINDOW], 0.0)
    landing = jnp.arange(blocks, dtype=jnp.int32)
    for distance in range(1, LAG + 1):
        mine = my_valid & (my_distance == distance)
        child_row = jnp.minimum(this_tok + distance, tok_count - 1)
        child_real = this_tok + distance < tok_count
        need = has_tail[child_row] & (distance_grid[child_row] == distance) & child_real
        arrived = return_each(jnp.where(mine[:, None], tail_grad, 0.0), distance)
        landing_map = (need[:, None] & (tail_local[child_row][:, None] == landing[None, :])).astype(
            jnp.float32
        )
        own_grad = own_grad + jnp.einsum(
            "eb,ex->bx", landing_map, arrived, precision=lax.Precision.HIGHEST
        )
    key_rows = own_grad[:, :lane_count].reshape(TOK_DEV, kv_dev * HEAD_DIM).astype(jnp.bfloat16)
    value_rows = own_grad[:, lane_count:].reshape(TOK_DEV, kv_dev * HEAD_DIM).astype(jnp.bfloat16)
    attended_rows = attended.reshape(TOK_DEV, kv_dev * group_size * HEAD_DIM)
    query_rows = query_grad.reshape(TOK_DEV, kv_dev * group_size * HEAD_DIM)
    attn_out, query_out, key_out, value_out = (
        lax.all_to_all(attended_rows, "head", split_axis=0, concat_axis=1, tiled=True),
        lax.all_to_all(query_rows, "head", split_axis=0, concat_axis=1, tiled=True),
        lax.all_to_all(key_rows, "head", split_axis=0, concat_axis=1, tiled=True),
        lax.all_to_all(value_rows, "head", split_axis=0, concat_axis=1, tiled=True),
    )
    sink_grad = lax.psum(jnp.sum(sink_parts, axis=0).reshape(kv_dev * group_size), "tok")
    return (attn_out, query_out, key_out, value_out, sink_grad)


def solution(mesh):
    return jax.shard_map(
        local,
        mesh=mesh,
        in_specs=(
            P(("tok", "head"), None),
            P(("tok", "head"), None),
            P(("tok", "head"), None),
            P(("tok", "head"), None),
            P("head"),
            P(),
            P(),
            P(),
        ),
        out_specs=(
            P(("tok", "head"), None),
            P(("tok", "head"), None),
            P(("tok", "head"), None),
            P(("tok", "head"), None),
            P("head"),
        ),
        check_vma=False,
    )
```

profile of v0, /device:TPU:8, one launch (start us, length us, event | category | flops | bytes accessed | tf_op | source)
XLA Modules:
  0.0 237.5 jit_solution(892521429869152023)
XLA Ops:
  0.6 1.8 copy.133
  2.4 5.5 %all-to-all-start = ((bf16[128,8,64]{0,2,1:T(8,128)(2,1)}), bf16[128,8,64]{0,2,1:T(8,128)(2,1)S(1)}, u32[]{:S(2)}, u32[]{:S(2)}) async-start(bf16[128,8,64]{0,2,1:T(8,128)(2,1)} %bitcast.70), calls=%async_computation | async-start | bytes 262144 | tf_op jit(solution)/shard_map/all_to_all | solution.py:107
  12.3 1.7 copy.134
  14.0 4.8 %all-to-all-start.1 = ((bf16[128,8,64]{0,2,1:T(8,128)(2,1)}), bf16[128,8,64]{0,2,1:T(8,128)(2,1)S(1)}, u32[]{:S(2)}, u32[]{:S(2)}) async-start(bf16[128,8,64]{0,2,1:T(8,128)(2,1)} %bitcast.74), calls=%async_computation.1 | async-start | bytes 262144 | tf_op jit(solution)/shard_map/all_to_all | solution.py:106
  19.1 2.3 copy.173
  21.3 1.3 copy.174
  23.5 4.9 %all-to-all-start.2 = ((bf16[128,8,512]{0,2,1:T(8,128)(2,1)}), bf16[128,8,512]{0,2,1:T(8,128)(2,1)S(1)}, u32[]{:S(2)}, u32[]{:S(2)}) async-start(bf16[128,8,512]{0,2,1:T(8,128)(2,1)} %bitcast.78), calls=%async_computation.2 | async-start | bytes 2097152 | tf_op jit(solution)/shard_map/all_to_all | solution.py:105
  30.9 6.0 %collective-permute-start = (bf16[2,16384]{1,0:T(2,128)(2,1)S(1)}, bf16[2,16384]{1,0:T(2,128)(2,1)S(1)}, u32[]{:S(2)}, u32[]{:S(2)}) collective-permute-start(bf16[2,16384]{1,0:T(2,128)(2,1)S(1)} %broadcast_select_fusion.9), channel_id=1, source_target_pairs={{0,24},{8,32},{16,40},{24,48},{32,56},{40,64},{48,72},{56,80},{64,... | collective-permute-start | bytes 196616 | tf_op jit(solution)/shard_map/ppermute | solution.py:18
  37.1 5.5 %collective-permute-start.1 = (bf16[2,16384]{1,0:T(2,128)(2,1)S(1)}, bf16[2,16384]{1,0:T(2,128)(2,1)S(1)}, u32[]{:S(2)}, u32[]{:S(2)}) collective-permute-start(bf16[2,16384]{1,0:T(2,128)(2,1)S(1)} %broadcast_select_fusion.8), channel_id=1, source_target_pairs={{0,16},{8,24},{16,32},{24,40},{32,48},{40,56},{48,64},{56,72},{64,... | collective-permute-start | bytes 196616 | tf_op jit(solution)/shard_map/ppermute | solution.py:18
  42.7 2.9 %collective-permute-start.2 = (bf16[2,16384]{1,0:T(2,128)(2,1)S(1)}, bf16[2,16384]{1,0:T(2,128)(2,1)S(1)}, u32[]{:S(2)}, u32[]{:S(2)}) collective-permute-start(bf16[2,16384]{1,0:T(2,128)(2,1)S(1)} %broadcast_select_fusion.5), channel_id=1, source_target_pairs={{0,8},{8,16},{16,24},{24,32},{32,40},{40,48},{48,56},{56,64},{64,7... | collective-permute-start | bytes 196616 | tf_op jit(solution)/shard_map/ppermute | solution.py:18
  45.7 2.4 %collective-permute-done.2 = bf16[2,16384]{1,0:T(2,128)(2,1)S(1)} collective-permute-done((bf16[2,16384]{1,0:T(2,128)(2,1)S(1)}, bf16[2,16384]{1,0:T(2,128)(2,1)S(1)}, u32[]{:S(2)}, u32[]{:S(2)}) %collective-permute-start.2) | collective-permute-done | bytes 65568 | tf_op jit(solution)/shard_map/ppermute | solution.py:18
  49.0 4.8 %all-to-all-start.3 = ((bf16[128,8,512]{0,2,1:T(8,128)(2,1)}), bf16[128,8,512]{0,2,1:T(8,128)(2,1)S(1)}, u32[]{:S(2)}, u32[]{:S(2)}) async-start(bf16[128,8,512]{0,2,1:T(8,128)(2,1)} %bitcast.99), calls=%async_computation.3 | async-start | bytes 2097152 | tf_op jit(solution)/shard_map/all_to_all | solution.py:108
  54.9 13.5 %all-to-all-done.3 = bf16[128,8,512]{0,2,1:T(8,128)(2,1)S(1)} async-done(((bf16[128,8,512]{0,2,1:T(8,128)(2,1)}), bf16[128,8,512]{0,2,1:T(8,128)(2,1)S(1)}, u32[]{:S(2)}, u32[]{:S(2)}) %all-to-all-start.3) | async-done | bytes 1048608 | tf_op jit(solution)/shard_map/all_to_all | solution.py:108
  68.4 22.1 %while.22 = (s32[]{:T(128)}, bf16[2,4,128,1,8,64]{2,5,4,1,3,0:T(8,128)(2,1)}, bf16[2,4,128,1,8,64]{2,5,4,1,3,0:T(8,128)(2,1)}, f32[2,4,128,1,64]{2,4,1,3,0:T(8,1...) while((s32[]{:T(128)}, ...), condition=%wide.region_12.13_spmd, body=%wide.region_5.12_spmd.sunk | while | flops 823066624 | bytes 67221672 | solution.py:166
  90.4 1.2 copy.149
  93.1 1.5 collective-permute-start.5
  95.5 1.3 collective-permute-start.3
  96.8 1.3 collective-permute-start.4
  98.1 3.9 %collective-permute-done.5 = f32[2,16384]{1,0:T(2,128)S(1)} collective-permute-done((f32[2,16384]{1,0:T(2,128)S(1)}, f32[2,16384]{1,0:T(2,128)S(1)}, u32[]{:S(2)}, u32[]{:S(2)}) %collective-permute-start.5) | collective-permute-done | bytes 131104 | tf_op jit(solution)/shard_map/ppermute | solution.py:18
  102.5 8.8 %collective-permute-done.4 = f32[2,16384]{1,0:T(2,128)S(1)} collective-permute-done((f32[2,16384]{1,0:T(2,128)S(1)}, f32[2,16384]{1,0:T(2,128)S(1)}, u32[]{:S(2)}, u32[]{:S(2)}) %collective-permute-start.4) | collective-permute-done | bytes 131104 | tf_op jit(solution)/shard_map/ppermute | solution.py:18
  113.5 4.7 %all-to-all-start.7 = ((bf16[8,128,64]{1,2,0:T(8,128)(2,1)}), bf16[8,128,64]{1,2,0:T(8,128)(2,1)S(1)}, u32[]{:S(2)}, u32[]{:S(2)}) async-start(bf16[8,128,64]{1,2,0:T(8,128)(2,1)} %copy.152), calls=%async_computation.7 | async-start | bytes 262144 | tf_op jit(solution)/shard_map/all_to_all | solution.py:210
  119.2 3.7 %all-to-all-done.7 = bf16[8,128,64]{1,2,0:T(8,128)(2,1)S(1)} async-done(((bf16[8,128,64]{1,2,0:T(8,128)(2,1)}), bf16[8,128,64]{1,2,0:T(8,128)(2,1)S(1)}, u32[]{:S(2)}, u32[]{:S(2)}) %all-to-all-start.7) | async-done | bytes 131104 | tf_op jit(solution)/shard_map/all_to_all | solution.py:210
  122.9 4.7 %all-to-all-start.6 = ((bf16[8,128,64]{1,2,0:T(8,128)(2,1)}), bf16[8,128,64]{1,2,0:T(8,128)(2,1)S(1)}, u32[]{:S(2)}, u32[]{:S(2)}) async-start(bf16[8,128,64]{1,2,0:T(8,128)(2,1)} %copy.151), calls=%async_computation.6 | async-start | bytes 262144 | tf_op jit(solution)/shard_map/all_to_all | solution.py:209
  127.6 1.3 copy.143
  129.0 3.4 %all-to-all-done.6 = bf16[8,128,64]{1,2,0:T(8,128)(2,1)S(1)} async-done(((bf16[8,128,64]{1,2,0:T(8,128)(2,1)}), bf16[8,128,64]{1,2,0:T(8,128)(2,1)S(1)}, u32[]{:S(2)}, u32[]{:S(2)}) %all-to-all-start.6) | async-done | bytes 131104 | tf_op jit(solution)/shard_map/all_to_all | solution.py:209
  132.3 4.9 %all-to-all-start.4 = ((bf16[8,128,512]{2,1,0:T(8,128)(2,1)}), bf16[8,128,512]{2,1,0:T(8,128)(2,1)S(1)}, u32[]{:S(2)}, u32[]{:S(2)}) async-start(bf16[8,128,512]{2,1,0:T(8,128)(2,1)} %copy.143), calls=%async_computation.4 | async-start | bytes 2097152 | tf_op jit(solution)/shard_map/all_to_all | solution.py:207
  137.3 1.3 copy.145
  138.6 13.2 %all-to-all-done.4 = bf16[8,128,512]{2,1,0:T(8,128)(2,1)S(1)} async-done(((bf16[8,128,512]{2,1,0:T(8,128)(2,1)}), bf16[8,128,512]{2,1,0:T(8,128)(2,1)S(1)}, u32[]{:S(2)}, u32[]{:S(2)}) %all-to-all-start.4) | async-done | bytes 1048608 | tf_op jit(solution)/shard_map/all_to_all | solution.py:207
  151.8 4.9 %all-to-all-start.5 = ((bf16[8,128,512]{2,1,0:T(8,128)(2,1)}), bf16[8,128,512]{2,1,0:T(8,128)(2,1)S(1)}, u32[]{:S(2)}, u32[]{:S(2)}) async-start(bf16[8,128,512]{2,1,0:T(8,128)(2,1)} %copy.145), calls=%async_computation.5 | async-start | bytes 2097152 | tf_op jit(solution)/shard_map/all_to_all | solution.py:208
  156.7 75.3 %psum.7 = f32[8]{0:T(128)} all-reduce(f32[8]{0:T(128)S(1)} %reduce_sum.73), channel_id=1, replica_groups=mesh['tok'=32,'head'=8] {'tok'}, use_global_device_ids=true, to_apply=%region_14.15 | all-reduce | flops 8 | bytes 64 | tf_op jit(solution)/shard_map/psum | solution.py:212
  234.2 1.3 copy.153
  236.2 1.3 copy.154
  (191 shorter events, 40.6 us)
Async XLA Ops:
  0.6 20.7 %copy-start = (bf16[128,4096]{1,0:T(8,128)(2,1)S(1)}, bf16[128,4096]{1,0:T(8,128)(2,1)}, u32[]{:S(2)}) copy-start(bf16[128,4096]{1,0:T(8,128)(2,1)} %param.13) | copy-start | bytes 3145732
  2.4 11.6 %all-to-all-start = ((bf16[128,8,64]{0,2,1:T(8,128)(2,1)}), bf16[128,8,64]{0,2,1:T(8,128)(2,1)S(1)}, u32[]{:S(2)}, u32[]{:S(2)}) async-start(bf16[128,8,64]{0,2,1:T(8,128)(2,1)} %bitcast.70), calls=%async_computation | async-start | bytes 262144 | tf_op jit(solution)/shard_map/all_to_all | solution.py:107
  14.0 9.5 %all-to-all-start.1 = ((bf16[128,8,64]{0,2,1:T(8,128)(2,1)}), bf16[128,8,64]{0,2,1:T(8,128)(2,1)S(1)}, u32[]{:S(2)}, u32[]{:S(2)}) async-start(bf16[128,8,64]{0,2,1:T(8,128)(2,1)} %bitcast.74), calls=%async_computation.1 | async-start | bytes 262144 | tf_op jit(solution)/shard_map/all_to_all | solution.py:106
  23.5 25.5 %all-to-all-start.2 = ((bf16[128,8,512]{0,2,1:T(8,128)(2,1)}), bf16[128,8,512]{0,2,1:T(8,128)(2,1)S(1)}, u32[]{:S(2)}, u32[]{:S(2)}) async-start(bf16[128,8,512]{0,2,1:T(8,128)(2,1)} %bitcast.78), calls=%async_computation.2 | async-start | bytes 2097152 | tf_op jit(solution)/shard_map/all_to_all | solution.py:105
  30.9 14.7 %collective-permute-start = (bf16[2,16384]{1,0:T(2,128)(2,1)S(1)}, bf16[2,16384]{1,0:T(2,128)(2,1)S(1)}, u32[]{:S(2)}, u32[]{:S(2)}) collective-permute-start(bf16[2,16384]{1,0:T(2,128)(2,1)S(1)} %broadcast_select_fusion.9), channel_id=1, source_target_pairs={{0,24},{8,32},{16,40},{24,48},{32,56},{40,64},{48,72},{56,80},{64,... | collective-permute-start | bytes 196616 | tf_op jit(solution)/shard_map/ppermute | solution.py:18
  37.1 8.6 %collective-permute-start.1 = (bf16[2,16384]{1,0:T(2,128)(2,1)S(1)}, bf16[2,16384]{1,0:T(2,128)(2,1)S(1)}, u32[]{:S(2)}, u32[]{:S(2)}) collective-permute-start(bf16[2,16384]{1,0:T(2,128)(2,1)S(1)} %broadcast_select_fusion.8), channel_id=1, source_target_pairs={{0,16},{8,24},{16,32},{24,40},{32,48},{40,56},{48,64},{56,72},{64,... | collective-permute-start | bytes 196616 | tf_op jit(solution)/shard_map/ppermute | solution.py:18
  42.7 5.4 %collective-permute-start.2 = (bf16[2,16384]{1,0:T(2,128)(2,1)S(1)}, bf16[2,16384]{1,0:T(2,128)(2,1)S(1)}, u32[]{:S(2)}, u32[]{:S(2)}) collective-permute-start(bf16[2,16384]{1,0:T(2,128)(2,1)S(1)} %broadcast_select_fusion.5), channel_id=1, source_target_pairs={{0,8},{8,16},{16,24},{24,32},{32,40},{40,48},{48,56},{56,64},{64,7... | collective-permute-start | bytes 196616 | tf_op jit(solution)/shard_map/ppermute | solution.py:18
  49.0 19.3 %all-to-all-start.3 = ((bf16[128,8,512]{0,2,1:T(8,128)(2,1)}), bf16[128,8,512]{0,2,1:T(8,128)(2,1)S(1)}, u32[]{:S(2)}, u32[]{:S(2)}) async-start(bf16[128,8,512]{0,2,1:T(8,128)(2,1)} %bitcast.99), calls=%async_computation.3 | async-start | bytes 2097152 | tf_op jit(solution)/shard_map/all_to_all | solution.py:108
  53.8 14.5 %copy-start.18 = (f32[8]{0:T(128)S(1)}, f32[8]{0:T(128)}, u32[]{:S(2)}) copy-start(f32[8]{0:T(128)} %param.14) | copy-start | bytes 100
  72.0 1.8 copy-start.13
  72.1 1.3 copy-start.4
  73.4 1.7 copy-start.8
  73.9 1.3 copy-start.5
  75.8 1.2 copy-start.1
  76.6 1.1 copy-start.10
  83.1 1.8 copy-start.13
  83.1 1.3 copy-start.4
  84.4 1.7 copy-start.8
  84.9 1.3 copy-start.5
  86.9 1.2 copy-start.1
  90.4 1.4 copy-start.9
  92.1 2.7 %copy-start.17 = (f32[2,4,128,1,64]{2,4,1,3,0:T(8,128)S(1)}, f32[2,4,128,1,64]{2,4,1,3,0:T(8,128)}, u32[]{:S(2)}) copy-start(f32[2,4,128,1,64]{2,4,1,3,0:T(8,128)} %get-tuple-element.100) | copy-start | bytes 786436
  92.3 2.9 %copy-start.14 = (f32[2,4,128,1,64]{2,4,1,3,0:T(8,128)S(1)}, f32[2,4,128,1,64]{2,4,1,3,0:T(8,128)}, u32[]{:S(2)}) copy-start(f32[2,4,128,1,64]{2,4,1,3,0:T(8,128)} %get-tuple-element.101) | copy-start | bytes 786436
  93.1 8.8 %collective-permute-start.5 = (f32[2,16384]{1,0:T(2,128)S(1)}, f32[2,16384]{1,0:T(2,128)S(1)}, u32[]{:S(2)}, u32[]{:S(2)}) collective-permute-start(f32[2,16384]{1,0:T(2,128)S(1)} %get-tuple-element.254), channel_id=1, source_target_pairs={{24,0},{32,8},{40,16},{48,24},{56,32},{64,40},{72,48},{80,56},{88,... | collective-permute-start | bytes 393224 | tf_op jit(solution)/shard_map/ppermute | solution.py:18
  95.5 16.3 %collective-permute-start.3 = (f32[2,16384]{1,0:T(2,128)S(1)}, f32[2,16384]{1,0:T(2,128)S(1)}, u32[]{:S(2)}, u32[]{:S(2)}) collective-permute-start(f32[2,16384]{1,0:T(2,128)S(1)} %get-tuple-element.252), channel_id=1, source_target_pairs={{8,0},{16,8},{24,16},{32,24},{40,32},{48,40},{56,48},{64,56},{72,6... | collective-permute-start | bytes 393224 | tf_op jit(solution)/shard_map/ppermute | solution.py:18
  96.8 14.5 %collective-permute-start.4 = (f32[2,16384]{1,0:T(2,128)S(1)}, f32[2,16384]{1,0:T(2,128)S(1)}, u32[]{:S(2)}, u32[]{:S(2)}) collective-permute-start(f32[2,16384]{1,0:T(2,128)S(1)} %get-tuple-element.253), channel_id=1, source_target_pairs={{16,0},{24,8},{32,16},{40,24},{48,32},{56,40},{64,48},{72,56},{80,... | collective-permute-start | bytes 393224 | tf_op jit(solution)/shard_map/ppermute | solution.py:18
  111.8 15.8 %copy-start.6 = (bf16[2,4,128,1,8,64]{2,5,4,1,3,0:T(8,128)(2,1)S(1)}, bf16[2,4,128,1,8,64]{2,5,4,1,3,0:T(8,128)(2,1)}, u32[]{:S(2)}) copy-start(bf16[2,4,128,1,8,64]{2,5,4,1,3,0:T(8,128)(2,1)} %get-tuple-element.98) | copy-start | bytes 3145732
  113.5 9.4 %all-to-all-start.7 = ((bf16[8,128,64]{1,2,0:T(8,128)(2,1)}), bf16[8,128,64]{1,2,0:T(8,128)(2,1)S(1)}, u32[]{:S(2)}, u32[]{:S(2)}) async-start(bf16[8,128,64]{1,2,0:T(8,128)(2,1)} %copy.152), calls=%async_computation.7 | async-start | bytes 262144 | tf_op jit(solution)/shard_map/all_to_all | solution.py:210
  122.9 9.4 %all-to-all-start.6 = ((bf16[8,128,64]{1,2,0:T(8,128)(2,1)}), bf16[8,128,64]{1,2,0:T(8,128)(2,1)S(1)}, u32[]{:S(2)}, u32[]{:S(2)}) async-start(bf16[8,128,64]{1,2,0:T(8,128)(2,1)} %copy.151), calls=%async_computation.6 | async-start | bytes 262144 | tf_op jit(solution)/shard_map/all_to_all | solution.py:209
  127.6 9.6 %copy-start.3 = (bf16[2,4,128,1,8,64]{2,5,4,1,3,0:T(8,128)(2,1)S(1)}, bf16[2,4,128,1,8,64]{2,5,4,1,3,0:T(8,128)(2,1)}, u32[]{:S(2)}) copy-start(bf16[2,4,128,1,8,64]{2,5,4,1,3,0:T(8,128)(2,1)} %get-tuple-element.99) | copy-start | bytes 3145732
  132.3 19.5 %all-to-all-start.4 = ((bf16[8,128,512]{2,1,0:T(8,128)(2,1)}), bf16[8,128,512]{2,1,0:T(8,128)(2,1)S(1)}, u32[]{:S(2)}, u32[]{:S(2)}) async-start(bf16[8,128,512]{2,1,0:T(8,128)(2,1)} %copy.143), calls=%async_computation.4 | async-start | bytes 2097152 | tf_op jit(solution)/shard_map/all_to_all | solution.py:207
  151.8 83.8 %all-to-all-start.5 = ((bf16[8,128,512]{2,1,0:T(8,128)(2,1)}), bf16[8,128,512]{2,1,0:T(8,128)(2,1)S(1)}, u32[]{:S(2)}, u32[]{:S(2)}) async-start(bf16[8,128,512]{2,1,0:T(8,128)(2,1)} %copy.145), calls=%async_computation.5 | async-start | bytes 2097152 | tf_op jit(solution)/shard_map/all_to_all | solution.py:208
  (13 other events, 12.2 us)
where the time goes:
time: 239 us; the launch traced here: 238 us
  blocking collectives  75.3 us (32%)
  starting transfers between devices  57.8 us (24%)
  waiting for transfers between devices  49.2 us (21%)
  local copies, waits for them, and re-layouts  31.3 us (13%)
  matrix products  13.1 us (5%)
  other arithmetic  9.39 us (4%)
    psum x1, blocking collectives, local(): lax.psum(jnp.sum(sink_parts, axis=0).reshape(kv_dev * group_size), 'tok')  75.3 us
    ppermute x6, starting transfers between devices, from_behind(): lax.ppermute(value, axis, [(source, source + steps) for source in range(l...  18.4 us
    ppermute x6, waiting for transfers between devices, from_behind(): lax.ppermute(value, axis, [(source, source + steps) for source in range(l...  15.1 us
    all_to_all x1, waiting for transfers between devices, local(): lax.all_to_all(out_grad, 'head', split_axis=1, concat_axis=0, tiled=True)  13.5 us
    all_to_all x1, waiting for transfers between devices, local(): lax.all_to_all(attended_rows, 'head', split_axis=0, concat_axis=1, tiled=...  13.2 us
    dot_general x24, matrix products, product(): return jnp.einsum(spec, left, right, preferred_element_type=jnp.float32)  11.5 us
    unnamed x22, local copies, waits for them, and re-layouts  7.64 us
    all_to_all x1, starting transfers between devices, local(): lax.all_to_all(value_states, 'head', split_axis=1, concat_axis=0, tiled=T...  5.47 us
  transfers between devices with their start and end apart: 14, of which 8 were waited for; matrix products, arithmetic and copies ran while one was open for 10% of the time, Pallas kernels for 0%

commit v1 on v0

v1 whole, which is shorter than its diff:
```python
import functools

import jax
import jax.numpy as jnp
from jax import lax
from jax.experimental import pallas as pl
from jax.experimental.pallas import tpu as pltpu
from jax.sharding import PartitionSpec as P

HEAD_DIM = 64
WINDOW = 128
LAG = 3
BR_DEV = 2
GROUP = 8
RING = 32
ROWS = WINDOW // GROUP
KV = 512
Z = 8
X = 4
F32 = jnp.float32
BF16 = jnp.bfloat16
MESH = pl.DeviceIdType.MESH


def place():
    return lax.axis_index("tok"), lax.axis_index("head")


def block_state(tok, head, start, length, parent):
    pos = (tok * GROUP + head) * WINDOW
    alive, opening = False, False
    for b in range(BR_DEV):
        first = start[tok * BR_DEV + b]
        covers = (first <= pos) & (pos < first + length[tok * BR_DEV + b])
        alive = alive | covers
        opening = opening | (covers & (first == pos))
    return alive, opening, parent[tok * BR_DEV, 0] >= 0


def tail_of(tok, start, parent):
    row = tok * BR_DEV
    token = start[jnp.maximum(parent[row, 0], 0)] + parent[row, 1]
    return lax.shift_right_logical(token, 10), lax.shift_right_logical(token, 7) & (GROUP - 1)


def send(src, dst, sems, slot, tok, head):
    copy = pltpu.make_async_remote_copy(
        src_ref=src,
        dst_ref=dst,
        send_sem=sems.at[0, slot],
        recv_sem=sems.at[1, slot],
        device_id=(tok, head),
        device_id_type=MESH,
    )
    copy.start()
    return copy


def meet(partners):
    barrier = pltpu.get_barrier_semaphore()
    for tok, head in partners:
        pl.semaphore_signal(barrier, inc=1, device_id=(tok, head), device_id_type=MESH)
    pl.semaphore_wait(barrier, len(partners))


def wrap(value, count):
    return lax.rem(value + count, count)


def fetch_kernel(
    start, length, parent, sink, key, value, prev, sinks,
    pair, a_buf, near, b_send, b_recv, mine, tail, tile, table,
    a_sems, s_sems, n_sems, b_sems, c_sems,
):
    tok, head = place()
    peers = [(tok, wrap(head + t, GROUP)) for t in range(1, GROUP)]
    later = [(wrap(tok + s, RING), head) for s in range(1, LAG + 1)]
    earlier = [(wrap(tok - s, RING), head) for s in range(1, LAG + 1)]
    meet(peers + later + earlier)

    pair[:, :, :KV] = key[...].reshape(GROUP, ROWS, KV)
    pair[:, :, KV:] = value[...].reshape(GROUP, ROWS, KV)
    row = lax.broadcasted_iota(jnp.int32, (8, 128), 0)
    sink_tile = jnp.zeros((8, 128), F32)
    for g in range(8):
        sink_tile = jnp.where(row == g, sink[g], sink_tile)
    tile[...] = sink_tile
    copies = []
    for t, (pt, ph) in enumerate(peers, 1):
        copies.append(send(pair.at[ph], a_buf.at[t], a_sems, t, pt, ph))
    near_copy = send(pair, near, n_sems, 0, tok, wrap(head + 1, GROUP))
    sink_copies = []
    for t, (pt, ph) in enumerate(peers, 1):
        sink_copies.append(send(tile, table.at[head], s_sems, t, pt, ph))
    table[head] = sink_tile
    a_buf[0] = pair[head]
    for copy in copies:
        copy.wait_recv()

    b_copies = []
    for s, (pt, ph) in enumerate(later, 1):
        _, local = tail_of(pt, start, parent)
        b_send[s - 1] = a_buf[(head - local) & (GROUP - 1)]
        b_copies.append(send(b_send.at[s - 1], b_recv.at[s - 1], b_sems, s - 1, pt, ph))
    owner, _ = tail_of(tok, start, parent)
    for copy in b_copies:
        copy.wait_recv()
    mine[...] = b_recv[jnp.clip(tok - owner - 1, 0, LAG - 1)]
    c_copies = []
    for t, (pt, ph) in enumerate(peers, 1):
        c_copies.append(send(mine, tail.at[head], c_sems, t, pt, ph))
    tail[head] = mine[...]
    alive, opening, rooted = block_state(tok, head, start, length, parent)
    ok = alive & (jnp.logical_not(opening) | rooted)
    near_copy.wait_recv()
    for copy in sink_copies:
        copy.wait_recv()
    sinks[...] = table[...].reshape(64, 128)
    for copy in c_copies:
        copy.wait_recv()
    chosen = jnp.where(opening, tail[...], near[...])
    prev[...] = jnp.where(ok, chosen, jnp.zeros_like(chosen)).reshape(WINDOW, 2 * KV)
    for copy in copies + [near_copy] + sink_copies + b_copies + c_copies:
        copy.wait_send()


def dot(left, right, dims):
    return lax.dot_general(left, right, (dims, ((), ())), preferred_element_type=F32)


def both_sides(block, lo):
    turned = pltpu.roll(block, HEAD_DIM, 1)
    zero = jnp.zeros_like(block)
    return (
        (jnp.where(lo, block, zero), jnp.where(lo, zero, turned)),
        (jnp.where(lo, turned, zero), jnp.where(lo, zero, block)),
    )


def join_sides(parts, lo):
    (a0, a1), (b0, b1) = parts
    return jnp.where(lo, a0, b1) + pltpu.roll(jnp.where(lo, b0, a1), HEAD_DIM, 1)


def attend_kernel(
    start, length, parent, query, grad, key, value, prev_key, prev_value, sinks,
    out, query_grad, own_k, own_v, prev_k, prev_v, sink_part,
):
    tok, head = place()
    alive, opening, rooted = block_state(tok, head, start, length, parent)
    ok = alive & (jnp.logical_not(opening) | rooted)
    lo = lax.broadcasted_iota(jnp.int32, (WINDOW, 128), 1) < HEAD_DIM
    place_j = lax.broadcasted_iota(jnp.int32, (WINDOW, 256), 0)
    place_i = lax.broadcasted_iota(jnp.int32, (WINDOW, 256), 1) & (WINDOW - 1)
    causal = place_j <= place_i
    bias = jnp.where(ok, 0.0, -jnp.inf)
    k_own = both_sides(key[...].astype(F32) * 0.125, lo)
    k_prev = both_sides(prev_key[...].astype(F32) * 0.125, lo)
    v_own = both_sides(value[...].astype(F32), lo)
    v_prev = both_sides(prev_value[...].astype(F32), lo)
    zero16 = jnp.zeros((WINDOW, 256), BF16)
    dks, dvs = [], []
    for c in range(2):
        k32 = [jnp.concatenate([k_own[c][e], k_prev[c][e]], 0) for e in range(2)]
        v32 = [jnp.concatenate([v_own[c][e], v_prev[c][e]], 0) for e in range(2)]
        k16 = [k.astype(BF16) for k in k32]
        v16 = [v.astype(BF16) for v in v32]
        k_turned = jnp.concatenate(k32, 0).T.astype(BF16)
        v_turned = jnp.concatenate(v32, 0).T.astype(BF16)
        dk = [jnp.zeros((256, 128), F32)] * 2
        dv = [jnp.zeros((256, 128), F32)] * 2
        for half in range(2):
            lanes = [512 * c + 256 * half + 128 * q for q in range(2)]
            q_rows = jnp.concatenate([query[:, at : at + 128] for at in lanes], 0)
            g_rows = jnp.concatenate([grad[:, at : at + 128] for at in lanes], 0)
            g_rows = jnp.where(alive, g_rows, jnp.zeros_like(g_rows))
            probs, slopes = [], []
            for e in range(2):
                heads = [8 * c + 4 * half + 2 * q + e for q in range(2)]
                scores = dot(k16[e], q_rows, ((1,), (1,)))
                scores = jnp.where(causal, scores[:WINDOW], scores[WINDOW:] + bias)
                inner = dot(v16[e], g_rows, ((1,), (1,)))
                inner = jnp.where(causal, inner[:WINDOW], inner[WINDOW:])
                sink = jnp.concatenate([sinks[h : h + 1, :] for h in heads], 1)
                peak = jnp.maximum(jnp.max(scores, axis=0, keepdims=True), sink)
                exps = jnp.exp(scores - peak)
                sink_exp = jnp.exp(sink - peak)
                inverse = 1.0 / (jnp.sum(exps, axis=0, keepdims=True) + sink_exp)
                prob = exps * inverse
                weighed = prob * inner
                delta = jnp.sum(weighed, axis=0, keepdims=True)
                slope = weighed - prob * delta
                term = sink_exp * inverse * delta
                for q, h in enumerate(heads):
                    sink_part[h : h + 1, :] = term[:, 128 * q : 128 * q + 128]
                prob16 = prob.astype(BF16)
                slope16 = slope.astype(BF16)
                prob2 = jnp.concatenate(
                    [jnp.where(causal, prob16, zero16), jnp.where(causal, zero16, prob16)], 0
                )
                slope2 = jnp.concatenate(
                    [jnp.where(causal, slope16, zero16), jnp.where(causal, zero16, slope16)], 0
                )
                dk[e] = dk[e] + dot(slope2, q_rows, ((1,), (0,)))
                dv[e] = dv[e] + dot(prob2, g_rows, ((1,), (0,)))
                probs.append(prob2)
                slopes.append(slope2)
            blended = dot(v_turned, jnp.concatenate(probs, 0), ((1,), (0,)))
            blended = jnp.where(alive, blended, jnp.zeros_like(blended))
            turned = dot(k_turned, jnp.concatenate(slopes, 0), ((1,), (0,)))
            for q, at in enumerate(lanes):
                out[:, at : at + 128] = blended[:, 128 * q : 128 * q + 128].T.astype(BF16)
                query_grad[:, at : at + 128] = turned[:, 128 * q : 128 * q + 128].T.astype(BF16)
        dks.append(dk)
        dvs.append(dv)
    own_k[...] = join_sides([[d[:WINDOW] for d in dk] for dk in dks], lo) * 0.125
    own_v[...] = join_sides([[d[:WINDOW] for d in dv] for dv in dvs], lo)
    prev_k[...] = (join_sides([[d[WINDOW:] for d in dk] for dk in dks], lo) * 0.125).astype(BF16)
    prev_v[...] = join_sides([[d[WINDOW:] for d in dv] for dv in dvs], lo).astype(BF16)


def give_kernel(
    start, length, parent, own_k, own_v, prev_k, prev_v, sink_part, key_grad, value_grad, sink_grad,
    tails, d_buf, near_send, near, e_send, e_recv, f_send, f_recv, s_send, s_recv, z_send, z_recv, x_send, x_recv,
    d_sems, s_sems, n_sems, e_sems, z_sems, f_sems, x_sems,
):
    tok, head = place()
    x, z = tok // Z, lax.rem(tok, Z)
    peers = [(tok, wrap(head + t, GROUP)) for t in range(1, GROUP)]
    later = [(wrap(tok + s, RING), head) for s in range(1, LAG + 1)]
    earlier = [(wrap(tok - s, RING), head) for s in range(1, LAG + 1)]
    z_peers = [(x * Z + wrap(z + t, Z), head) for t in range(1, Z)]
    x_peers = [(wrap(x + t, X) * Z + z, head) for t in range(1, X)]
    meet(peers + later + earlier + z_peers + x_peers)
    alive, opening, rooted = block_state(tok, head, start, length, parent)
    outward = opening & rooted
    inward = alive & jnp.logical_not(opening)
    for part, ref in enumerate((prev_k, prev_v)):
        block = ref[...].reshape(GROUP, ROWS, KV)
        lanes = slice(part * KV, part * KV + KV)
        tails[:, :, lanes] = jnp.where(outward, block, jnp.zeros_like(block))
        near_send[:, :, lanes] = jnp.where(inward, block, jnp.zeros_like(block))
    s_send[...] = sink_part[...].reshape(GROUP, 8, 128)
    copies, sink_copies = [], []
    for t, (pt, ph) in enumerate(peers, 1):
        copies.append(send(tails.at[ph], d_buf.at[t], d_sems, t, pt, ph))
    for t, (pt, ph) in enumerate(peers, 1):
        sink_copies.append(send(s_send.at[ph], s_recv.at[t], s_sems, t, pt, ph))
    near_copy = send(near_send, near, n_sems, 0, tok, wrap(head - 1, GROUP))
    total = tails[head].astype(F32)
    for t, copy in enumerate(copies, 1):
        copy.wait_recv()
        total = total + d_buf[t].astype(F32)
    owner, _ = tail_of(tok, start, parent)
    e_copies = []
    for s, (pt, ph) in enumerate(earlier, 1):
        e_send[s - 1] = jnp.where(tok - owner == s, total, jnp.zeros_like(total)).astype(BF16)
        e_copies.append(send(e_send.at[s - 1], e_recv.at[s - 1], e_sems, s - 1, pt, ph))
    sink_sum = s_send[head]
    for t, copy in enumerate(sink_copies, 1):
        copy.wait_recv()
        sink_sum = sink_sum + s_recv[t]
    z_send[...] = sink_sum
    z_copies = []
    for t, (pt, ph) in enumerate(z_peers, 1):
        z_copies.append(send(z_send, z_recv.at[t], z_sems, t, pt, ph))
    for copy in e_copies:
        copy.wait_recv()
    locals_ = [tail_of(pt, start, parent)[1] for pt, _ in later]
    arrived = [e_recv[s].astype(F32) for s in range(LAG)]
    f_copies = []

    def landed(place_):
        landing = jnp.zeros((ROWS, 2 * KV), F32)
        for s in range(LAG):
            landing = landing + jnp.where(locals_[s] == place_, arrived[s], 0.0)
        return landing.astype(BF16)

    for t, (pt, ph) in enumerate(peers, 1):
        f_send[t] = landed(ph)
        f_copies.append(send(f_send.at[t], f_recv.at[head], f_sems, t, pt, ph))
    f_recv[head] = landed(head)
    for t, copy in enumerate(z_copies, 1):
        copy.wait_recv()
        sink_sum = sink_sum + z_recv[t]
    x_send[...] = sink_sum
    x_copies = []
    for t, (pt, ph) in enumerate(x_peers, 1):
        x_copies.append(send(x_send, x_recv.at[t], x_sems, t, pt, ph))
    near_copy.wait_recv()
    for copy in f_copies:
        copy.wait_recv()
    back = f_recv[...].astype(F32) + near[...].astype(F32)
    back = back.reshape(WINDOW, 2 * KV)
    key_grad[...] = (own_k[...] + back[:, :KV]).astype(BF16)
    value_grad[...] = (own_v[...] + back[:, KV:]).astype(BF16)
    for t, copy in enumerate(x_copies, 1):
        copy.wait_recv()
        sink_sum = sink_sum + x_recv[t]
    sums = jnp.sum(sink_sum, axis=1, keepdims=True)
    row = lax.broadcasted_iota(jnp.int32, (8, 128), 0)
    lane = lax.broadcasted_iota(jnp.int32, (8, 128), 1)
    line = jnp.sum(jnp.where(row == lane, sums, 0.0), axis=0)
    sink_grad[...] = -line[:8]
    for copy in copies + sink_copies + [near_copy] + e_copies + z_copies + f_copies + x_copies:
        copy.wait_send()


SMEM = pl.BlockSpec(memory_space=pltpu.SMEM)
VMEM = pl.BlockSpec(memory_space=pltpu.VMEM)
DMA = pltpu.SemaphoreType.DMA


def local(queries, key_states, value_states, out_grad, sink_logits, branch_start, branch_len, parent_list):
    slices = (GROUP, ROWS, 2 * KV)
    one = (ROWS, 2 * KV)
    prev, sinks = pl.pallas_call(
        fetch_kernel,
        name="fetch",
        out_shape=(
            jax.ShapeDtypeStruct((WINDOW, 2 * KV), BF16),
            jax.ShapeDtypeStruct((64, 128), F32),
        ),
        in_specs=[SMEM] * 4 + [VMEM] * 2,
        out_specs=(VMEM, VMEM),
        scratch_shapes=[
            pltpu.VMEM(slices, BF16),
            pltpu.VMEM(slices, BF16),
            pltpu.VMEM(slices, BF16),
            pltpu.VMEM((LAG,) + one, BF16),
            pltpu.VMEM((LAG,) + one, BF16),
            pltpu.VMEM(one, BF16),
            pltpu.VMEM(slices, BF16),
            pltpu.VMEM((8, 128), F32),
            pltpu.VMEM((GROUP, 8, 128), F32),
            DMA((2, GROUP)),
            DMA((2, GROUP)),
            DMA((2, 1)),
            DMA((2, LAG)),
            DMA((2, GROUP)),
        ],
        compiler_params=pltpu.CompilerParams(collective_id=0, has_side_effects=True),
    )(branch_start, branch_len, parent_list, sink_logits, key_states, value_states)

    wide = pl.BlockSpec((WINDOW, 1024), lambda p: (0, p))
    narrow = pl.BlockSpec((WINDOW, 128), lambda p: (0, p))
    narrow_v = pl.BlockSpec((WINDOW, 128), lambda p: (0, p + 4))
    lines = pl.BlockSpec((16, 128), lambda p: (p, 0))
    attn_out, query_grad, own_k, own_v, prev_k, prev_v, sink_part = pl.pallas_call(
        attend_kernel,
        name="attend",
        grid=(4,),
        out_shape=(
            jax.ShapeDtypeStruct((WINDOW, 4096), BF16),
            jax.ShapeDtypeStruct((WINDOW, 4096), BF16),
            jax.ShapeDtypeStruct((WINDOW, KV), F32),
            jax.ShapeDtypeStruct((WINDOW, KV), F32),
            jax.ShapeDtypeStruct((WINDOW, KV), BF16),
            jax.ShapeDtypeStruct((WINDOW, KV), BF16),
            jax.ShapeDtypeStruct((64, 128), F32),
        ),
        in_specs=[SMEM] * 3 + [wide, wide, narrow, narrow, narrow, narrow_v, lines],
        out_specs=(wide, wide, narrow, narrow, narrow, narrow, lines),
        compiler_params=pltpu.CompilerParams(vmem_limit_bytes=48 * 1024 * 1024),
    )(branch_start, branch_len, parent_list, queries, out_grad, key_states, value_states, prev, prev, sinks)

    key_grad, value_grad, sink_grad = pl.pallas_call(
        give_kernel,
        name="give",
        out_shape=(
            jax.ShapeDtypeStruct((WINDOW, KV), BF16),
            jax.ShapeDtypeStruct((WINDOW, KV), BF16),
            jax.ShapeDtypeStruct((8,), F32),
        ),
        in_specs=[SMEM] * 3 + [VMEM] * 5,
        out_specs=(VMEM, VMEM, VMEM),
        scratch_shapes=[
            pltpu.VMEM(slices, BF16),
            pltpu.VMEM(slices, BF16),
            pltpu.VMEM(slices, BF16),
            pltpu.VMEM(slices, BF16),
            pltpu.VMEM((LAG,) + one, BF16),
            pltpu.VMEM((LAG,) + one, BF16),
            pltpu.VMEM(slices, BF16),
            pltpu.VMEM(slices, BF16),
            pltpu.VMEM((GROUP, 8, 128), F32),
            pltpu.VMEM((GROUP, 8, 128), F32),
            pltpu.VMEM((8, 128), F32),
            pltpu.VMEM((Z, 8, 128), F32),
            pltpu.VMEM((8, 128), F32),
            pltpu.VMEM((X, 8, 128), F32),
            DMA((2, GROUP)),
            DMA((2, GROUP)),
            DMA((2, 1)),
            DMA((2, LAG)),
            DMA((2, Z)),
            DMA((2, GROUP)),
            DMA((2, X)),
        ],
        compiler_params=pltpu.CompilerParams(collective_id=1, has_side_effects=True),
    )(branch_start, branch_len, parent_list, own_k, own_v, prev_k, prev_v, sink_part)
    return attn_out, query_grad, key_grad, value_grad, sink_grad


def solution(mesh):
    rows = P(("tok", "head"), None)
    return jax.shard_map(
        local,
        mesh=mesh,
        in_specs=(rows, rows, rows, rows, P("head"), P(), P(), P()),
        out_specs=(rows, rows, rows, rows, P("head")),
        check_vma=False,
    )
```

time: 239 us -> 81.2 us (0.34)
  the two profiles are of different devices: /device:TPU:8 before, /device:TPU:1 now
where the time goes in v1:
time: 81.2 us; the launch traced here: 79.7 us
  Pallas kernels  66.7 us (82%)
  local copies, waits for them, and re-layouts  12.3 us (15%)
    pallas_call x1, Pallas kernels, local(): pl.pallas_call(fetch_kernel, name='fetch', out_shape=(jax.ShapeDtypeStruc...  31.7 us
    pallas_call x1, Pallas kernels, local(): pl.pallas_call(give_kernel, name='give', out_shape=(jax.ShapeDtypeStruct(...  20.7 us
    pallas_call x1, Pallas kernels, local(): pl.pallas_call(attend_kernel, name='attend', grid=(4,), out_shape=(jax.Sh...  14.3 us
    unnamed x36, local copies, waits for them, and re-layouts  12.3 us

profile of v1, /device:TPU:1, one launch (start us, length us, event | category | flops | bytes accessed | tf_op | source)
XLA Modules:
  0.0 79.7 jit_solution(8882665238011961582)
XLA Ops:
  0.6 1.4 %copy.14.parent = s32[64,2]{1,0:T(8,128)} copy(s32[64,2]{0,1:T(2,128)} %param.15) | data formatting | bytes 1024 | tf_op args[7]
  2.0 0.0 copy-start.3
  2.0 0.0 copy-start.4
  2.0 0.0 copy-start.5
  2.0 31.7 %fetch.1 = (bf16[128,1024]{1,0:T(8,128)(2,1)}, f32[64,128]{1,0:T(8,128)}) custom-call(s32[64]{0:T(128)} %start.5, s32[64]{0:T(128)} %length.5, s32[64,2]{1,0:T(8,128)} %copy.14.parent, f32[8]{0:T(128)} %sink.1, bf16[128,512]{1,0:T(8,128)(2,1)} %key.3, bf16[128,512]{1,0:T(8,128)(2,1)} %value.3), custom_call_target="tpu_custom_call" | custom-call | tf_op jit(solution)/shard_map/fetch/pallas_call | solution.py:317
  33.7 0.0 copy-start.12
  33.7 0.0 copy-start.13
  33.7 0.0 copy-done.3
  33.7 0.0 copy-done.4
  33.7 0.0 copy-done.5
  33.8 0.6 copy-done.12
  34.4 0.0 copy-done.13
  34.4 0.0 copy-start
  34.4 1.2 %copy-done = bf16[128,4096]{1,0:T(8,128)(2,1)S(1)} copy-done((bf16[128,4096]{1,0:T(8,128)(2,1)S(1)}, bf16[128,4096]{1,0:T(8,128)(2,1)}, u32[]{:S(2)}) %copy-start) | copy-done | bytes 1048600
  35.6 0.0 copy-start.1
  35.6 1.2 %copy-done.1 = bf16[128,4096]{1,0:T(8,128)(2,1)S(1)} copy-done((bf16[128,4096]{1,0:T(8,128)(2,1)S(1)}, bf16[128,4096]{1,0:T(8,128)(2,1)}, u32[]{:S(2)}) %copy-start.1) | copy-done | bytes 1048600
  36.8 0.0 copy-start.2
  36.8 0.9 %copy-done.2 = bf16[128,1024]{1,0:T(8,128)(2,1)S(1)} copy-done((bf16[128,1024]{1,0:T(8,128)(2,1)S(1)}, bf16[128,1024]{1,0:T(8,128)(2,1)}, u32[]{:S(2)}) %copy-start.2) | copy-done | bytes 262168
  37.8 0.8 copy-done.10
  38.5 14.3 %attend.1 = (bf16[128,4096]{1,0:T(8,128)(2,1)}, bf16[128,4096]{1,0:T(8,128)(2,1)}, f32[128,512]{1,0:T(8,128)S(1)}, f32[128,512]{1,0:T(8,128)S(1)}, bf16[128,512]...) custom-call(s32[64]{0:T(128)S(1)} %copy-done.12, s32[64]{0:T(128)S(1)} %copy-done.13, ...), custom_call_target="tpu_custom_call" | custom-call | tf_op jit(solution)/shard_map/attend/pallas_call | solution.py:349
  52.9 0.7 copy-done.6
  53.6 0.7 copy-done.7
  54.3 0.7 copy-done.8
  54.9 0.7 copy-done.9
  55.6 0.6 copy-done.11
  56.2 20.7 %give.1 = (bf16[128,512]{1,0:T(8,128)(2,1)}, bf16[128,512]{1,0:T(8,128)(2,1)}, f32[8]{0:T(128)}) custom-call(s32[64]{0:T(128)} %start.5, s32[64]{0:T(128)} %length.5, s32[64,2]{1,0:T(8,128)} %copy.14.parent, f32[128,512]{1,0:T(8,128)} %copy-done.6, f32[128,512]{1,0:T(8,128)} %copy-done.7, bf16[128,512]{1,0:T(8,128)(2,1)} %copy-done.8, ...), custom_call_target="tpu_custom_call" | custom-call | tf_op jit(solution)/shard_map/give/pallas_call | solution.py:367
  76.9 0.0 copy-start.14
  76.9 1.6 %copy.19 = bf16[128,512]{1,0:T(8,128)(2,1)} copy(bf16[128,512]{1,0:T(8,128)(2,1)} %get-tuple-element.36) | data formatting | bytes 262144
  78.5 0.0 copy-done.14
  78.5 0.7 copy.20
  79.2 0.0 copy-done.15
  79.2 0.5 copy.21
  (7 shorter events, 0.0 us)
Async XLA Ops:
  2.0 31.7 %copy-start.3 = (s32[64,2]{1,0:T(8,128)S(1)}, s32[64,2]{1,0:T(8,128)}, u32[]{:S(2)}) copy-start(s32[64,2]{1,0:T(8,128)} %copy.14.parent) | copy-start | bytes 1540
  2.0 31.7 %copy-start.4 = (bf16[128,512]{1,0:T(8,128)(2,1)S(1)}, bf16[128,512]{1,0:T(8,128)(2,1)}, u32[]{:S(2)}) copy-start(bf16[128,512]{1,0:T(8,128)(2,1)} %key.3) | copy-start | bytes 393220
  2.0 31.7 %copy-start.5 = (bf16[128,512]{1,0:T(8,128)(2,1)S(1)}, bf16[128,512]{1,0:T(8,128)(2,1)}, u32[]{:S(2)}) copy-start(bf16[128,512]{1,0:T(8,128)(2,1)} %value.3) | copy-start | bytes 393220
  33.7 0.7 copy-start.12
  33.7 0.7 copy-start.13
  34.4 1.2 %copy-start = (bf16[128,4096]{1,0:T(8,128)(2,1)S(1)}, bf16[128,4096]{1,0:T(8,128)(2,1)}, u32[]{:S(2)}) copy-start(bf16[128,4096]{1,0:T(8,128)(2,1)} %query.1) | copy-start | bytes 3145732
  35.6 1.2 %copy-start.1 = (bf16[128,4096]{1,0:T(8,128)(2,1)S(1)}, bf16[128,4096]{1,0:T(8,128)(2,1)}, u32[]{:S(2)}) copy-start(bf16[128,4096]{1,0:T(8,128)(2,1)} %grad.1) | copy-start | bytes 3145732
  36.8 0.9 %copy-start.2 = (bf16[128,1024]{1,0:T(8,128)(2,1)S(1)}, bf16[128,1024]{1,0:T(8,128)(2,1)}, u32[]{:S(2)}) copy-start(bf16[128,1024]{1,0:T(8,128)(2,1)} %get-tuple-element.17.prev_key.prev_value) | copy-start | bytes 786436
  37.8 0.8 copy-start.10
  52.9 0.7 copy-start.6
  53.6 0.7 copy-start.7
  54.3 0.7 copy-start.8
  54.9 0.7 copy-start.9
  55.6 0.6 copy-start.11
  76.9 1.6 %copy-start.14 = (bf16[128,512]{1,0:T(8,128)(2,1)S(1)}, bf16[128,512]{1,0:T(8,128)(2,1)}, u32[]{:S(2)}) copy-start(bf16[128,512]{1,0:T(8,128)(2,1)} %get-tuple-element.37) | copy-start | bytes 393220
  78.5 0.7 copy-start.15

commit v2 on v1

v2 whole, which is shorter than its diff:
```python
import jax
import jax.numpy as jnp
from jax import lax
from jax.experimental import pallas as pl
from jax.experimental.pallas import tpu as pltpu
from jax.sharding import PartitionSpec as P

HEAD_DIM = 64
WINDOW = 128
LAG = 3
PAIRS = 4
BR_DEV = 2
GROUP = 8
RING = 32
ROWS = WINDOW // GROUP
KV = 512
Z = 8
X = 4
F32 = jnp.float32
BF16 = jnp.bfloat16
MESH = pl.DeviceIdType.MESH


def place():
    return lax.axis_index("tok"), lax.axis_index("head")


def block_state(tok, head, start, length, parent):
    pos = (tok * GROUP + head) * WINDOW
    alive, opening = False, False
    for b in range(BR_DEV):
        first = start[tok * BR_DEV + b]
        covers = (first <= pos) & (pos < first + length[tok * BR_DEV + b])
        alive = alive | covers
        opening = opening | (covers & (first == pos))
    return alive, opening, parent[0, tok * BR_DEV] >= 0


def tail_of(tok, start, parent):
    row = tok * BR_DEV
    token = start[jnp.maximum(parent[0, row], 0)] + parent[1, row]
    return lax.shift_right_logical(token, 10), lax.shift_right_logical(token, 7) & (GROUP - 1)


def send(src, dst, sems, slot, tok, head):
    copy = pltpu.make_async_remote_copy(
        src_ref=src,
        dst_ref=dst,
        send_sem=sems.at[0, slot],
        recv_sem=sems.at[1, slot],
        device_id=(tok, head),
        device_id_type=MESH,
    )
    copy.start()
    return copy


def wrap(value, count):
    return lax.rem(value + count, count)


def dot(left, right, dims):
    return lax.dot_general(left, right, (dims, ((), ())), preferred_element_type=F32)


def both_sides(block, lo):
    turned = pltpu.roll(block, HEAD_DIM, 1)
    zero = jnp.zeros_like(block)
    return (
        (jnp.where(lo, block, zero), jnp.where(lo, zero, turned)),
        (jnp.where(lo, turned, zero), jnp.where(lo, zero, block)),
    )


def join_sides(parts, lo):
    (a0, a1), (b0, b1) = parts
    return jnp.where(lo, a0, b1) + pltpu.roll(jnp.where(lo, b0, a1), HEAD_DIM, 1)


FAR_FIRST = (4, 5, 3, 6, 2, 7, 1)


def split_rows(rows):
    high = rows.astype(BF16).astype(F32)
    return jnp.concatenate([high, rows - high], 1).astype(BF16)


def kernel(
    start, length, parent, sink, queries, out_grad, keys, values,
    attn_out, query_grad, key_grad, value_grad, sink_grad,
    query, grad, out, turned_out, pair, a_buf, near, b_send, b_recv, mine, tail, prev, table,
    s_own, p_own, probs, slopes, own_k, own_v,
    give, d_buf, near_send, near_back, e_send, e_recv, f_send, f_recv, z_send, z_recv, x_send, x_recv, part,
    load_sems, store_sems, a_sems, n_sems, b_sems, c_sems, d_sems, e_sems, f_sems, z_sems, x_sems,
):
    tok, head = place()
    x, z = tok // Z, lax.rem(tok, Z)
    peers = [(t, (tok, wrap(head + t, GROUP))) for t in FAR_FIRST]
    later = [(s, (wrap(tok + s, RING), head)) for s in (3, 2, 1)]
    earlier = [(s, (wrap(tok - s, RING), head)) for s in (3, 2, 1)]
    z_peers = [(t, (x * Z + wrap(z + t, Z), head)) for t in FAR_FIRST]
    x_peers = [(t, (wrap(x + t, X) * Z + z, head)) for t in (2, 3, 1)]
    right, left = (tok, wrap(head + 1, GROUP)), (tok, wrap(head - 1, GROUP))

    loads = [
        pltpu.make_async_copy(src, dst, load_sems.at[n])
        for n, (src, dst) in enumerate((
            (keys, pair.at[:, pl.ds(0, KV)]), (values, pair.at[:, pl.ds(KV, KV)]), (queries, query), (out_grad, grad),
        ))
    ]
    for load in loads:
        load.start()
    barrier = pltpu.get_barrier_semaphore()
    partners = [who for _, who in z_peers + later + earlier + peers + x_peers]
    for who in partners:
        pl.semaphore_signal(barrier, inc=1, device_id=who, device_id_type=MESH)

    alive, opening, rooted = block_state(tok, head, start, length, parent)
    ok = alive & (jnp.logical_not(opening) | rooted)
    outward = opening & rooted
    inward = alive & jnp.logical_not(opening)
    row = lax.broadcasted_iota(jnp.int32, (8, 128), 0)
    lane = lax.broadcasted_iota(jnp.int32, (8, 128), 1)
    sink_tile = jnp.zeros((8, 128), F32)
    for g in range(8):
        sink_tile = jnp.where(row == g, sink[g], sink_tile)
    table[head] = sink_tile
    pair[:, 2 * KV :] = split_rows(jnp.broadcast_to(sink_tile[None], (GROUP, 8, 128))).reshape(WINDOW, 128)
    loads[0].wait()
    loads[1].wait()
    pl.semaphore_wait(barrier, len(partners))

    def rows_of(place_):
        return pl.ds(pl.multiple_of(place_ * ROWS, ROWS), ROWS)

    sent = []

    def ship(src, dst, sems, slot, who):
        copy = send(src, dst, sems, slot, *who)
        sent.append(copy)
        return copy

    a_copies = [(t, ship(pair.at[rows_of(who[1])], a_buf.at[t], a_sems, t, who)) for t, who in peers]
    near_copy = ship(pair.at[:, pl.ds(0, 2 * KV)], near, n_sems, 0, right)
    a_buf[0] = pair[rows_of(head), :]

    lo = lax.broadcasted_iota(jnp.int32, (WINDOW, 128), 1) < HEAD_DIM
    place_j = lax.broadcasted_iota(jnp.int32, (WINDOW, 256), 0)
    place_i = lax.broadcasted_iota(jnp.int32, (WINDOW, 256), 1) & (WINDOW - 1)
    causal = place_j <= place_i
    causal16 = causal.astype(F32).astype(BF16)
    bias = jnp.where(ok, 0.0, -jnp.inf)

    def lanes_at(at, size=128):
        return pl.ds(pl.multiple_of(at, size), size)

    def sides(ref, p, factor):
        k = both_sides(ref[:, lanes_at(p * 128)].astype(F32) * factor, lo)
        v = both_sides(ref[:, lanes_at(KV + p * 128)].astype(F32), lo)
        return k, v

    def stacked(ref, at):
        return jnp.concatenate([ref[:, lanes_at(at)], ref[:, lanes_at(at + 128)]], 0)

    def before(p, carry):
        wide = lanes_at(p * 1024, 1024)
        grad[:, wide] = jnp.where(alive, grad[:, wide], jnp.zeros((), BF16))
        k, v = sides(pair, p, 0.125)
        for c in range(2):
            for half in range(2):
                at = p * 1024 + 512 * c + 256 * half
                q_rows, g_rows = stacked(query, at), stacked(grad, at)
                for e in range(2):
                    unit = 4 * c + 2 * half + e
                    s_own[p, unit] = dot(k[c][e].astype(BF16), q_rows, ((1,), (1,)))
                    p_own[p, unit] = dot(v[c][e].astype(BF16), g_rows, ((1,), (1,)))
        return carry

    loads[2].wait()
    loads[3].wait()
    lax.fori_loop(0, PAIRS, before, 0)

    for t, copy in a_copies:
        copy.wait_recv()
    b_copies = []
    for s, who in later:
        _, place_ = tail_of(who[0], start, parent)
        b_send[s - 1] = a_buf[(head - place_) & (GROUP - 1)][:, : 2 * KV]
        b_copies.append(ship(b_send.at[s - 1], b_recv.at[s - 1], b_sems, s - 1, who))
    for t in range(1, GROUP):
        extra = a_buf[t, :, 2 * KV :].astype(F32)
        table[wrap(head - t, GROUP)] = extra[:8] + extra[8:]
    owner, _ = tail_of(tok, start, parent)
    for copy in b_copies:
        copy.wait_recv()
    mine[...] = b_recv[jnp.clip(tok - owner - 1, 0, LAG - 1)]
    c_copies = [ship(mine, tail.at[rows_of(head)], c_sems, t, who) for t, who in peers]
    tail[rows_of(head), :] = mine[...]
    near_copy.wait_recv()
    for copy in c_copies:
        copy.wait_recv()
    prev[...] = jnp.where(ok, jnp.where(opening, tail[...], near[...]), jnp.zeros((), BF16))

    def during(p, carry):
        k, v = sides(prev, p, 0.125)
        dks, dvs = [], []
        for c in range(2):
            dk = [jnp.zeros((WINDOW, 128), F32)] * 2
            dv = [jnp.zeros((WINDOW, 128), F32)] * 2
            for half in range(2):
                at = p * 1024 + 512 * c + 256 * half
                q_rows, g_rows = stacked(query, at), stacked(grad, at)
                for e in range(2):
                    unit = 4 * c + 2 * half + e
                    lines = [4 * half + 2 * q + e for q in range(2)]
                    scores = dot(k[c][e].astype(BF16), q_rows, ((1,), (1,)))
                    scores = jnp.where(causal, s_own[p, unit], scores + bias)
                    inner = dot(v[c][e].astype(BF16), g_rows, ((1,), (1,)))
                    inner = jnp.where(causal, p_own[p, unit], inner)
                    sinks = jnp.concatenate([table[2 * p + c, h : h + 1, :] for h in lines], 1)
                    peak = jnp.maximum(jnp.max(scores, axis=0, keepdims=True), sinks)
                    exps = jnp.exp(scores - peak)
                    sink_exp = jnp.exp(sinks - peak)
                    inverse = 1.0 / (jnp.sum(exps, axis=0, keepdims=True) + sink_exp)
                    prob = exps * inverse
                    weighed = prob * inner
                    delta = jnp.sum(weighed, axis=0, keepdims=True)
                    slope = weighed - prob * delta
                    term = sink_exp * inverse * delta
                    for q, h in enumerate(lines):
                        part[2 * p + c, h : h + 1, :] = term[:, 128 * q : 128 * q + 128]
                    prob16 = prob.astype(BF16)
                    slope16 = slope.astype(BF16)
                    probs[p, unit] = prob16
                    slopes[p, unit] = slope16
                    dk[e] = dk[e] + dot(slope16 - slope16 * causal16, q_rows, ((1,), (0,)))
                    dv[e] = dv[e] + dot(prob16 - prob16 * causal16, g_rows, ((1,), (0,)))
            dks.append(dk)
            dvs.append(dv)
        zero16 = jnp.zeros((), BF16)
        for at, block in ((p * 128, join_sides(dks, lo) * 0.125), (KV + p * 128, join_sides(dvs, lo))):
            block = block.astype(BF16)
            give[:, lanes_at(at)] = jnp.where(outward, block, zero16)
            near_send[:, lanes_at(at)] = jnp.where(inward, block, zero16)
        return carry

    lax.fori_loop(0, PAIRS, during, 0)
    give[:, 2 * KV :] = split_rows(part[...]).reshape(WINDOW, 128)

    d_copies = [(t, ship(give.at[rows_of(who[1])], d_buf.at[t], d_sems, t, who)) for t, who in peers]
    back_copy = ship(near_send, near_back, n_sems, 1, left)

    def stores(p):
        wide = lanes_at(p * 1024, 1024)
        return (
            pltpu.make_async_copy(out.at[:, wide], attn_out.at[:, wide], store_sems.at[0, p]),
            pltpu.make_async_copy(turned_out.at[:, wide], query_grad.at[:, wide], store_sems.at[1, p]),
        )

    def after(p, carry):
        k_own, v_own = sides(pair, p, 0.125)
        k_prev, v_prev = sides(prev, p, 0.125)
        dks, dvs = [], []
        for c in range(2):
            k_all = jnp.concatenate([k_own[c][0], k_prev[c][0], k_own[c][1], k_prev[c][1]], 0)
            v_all = jnp.concatenate([v_own[c][0], v_prev[c][0], v_own[c][1], v_prev[c][1]], 0)
            k_turned = k_all.T.astype(BF16)
            v_turned = v_all.T.astype(BF16)
            dk = [jnp.zeros((WINDOW, 128), F32)] * 2
            dv = [jnp.zeros((WINDOW, 128), F32)] * 2
            for half in range(2):
                at = p * 1024 + 512 * c + 256 * half
                q_rows, g_rows = stacked(query, at), stacked(grad, at)
                prob_all, slope_all = [], []
                for e in range(2):
                    unit = 4 * c + 2 * half + e
                    prob16, slope16 = probs[p, unit], slopes[p, unit]
                    prob_own, slope_own = prob16 * causal16, slope16 * causal16
                    dk[e] = dk[e] + dot(slope_own, q_rows, ((1,), (0,)))
                    dv[e] = dv[e] + dot(prob_own, g_rows, ((1,), (0,)))
                    prob_all += [prob_own, prob16 - prob_own]
                    slope_all += [slope_own, slope16 - slope_own]
                blended = dot(v_turned, jnp.concatenate(prob_all, 0), ((1,), (0,)))
                blended = jnp.where(alive, blended, 0.0)
                turned = dot(k_turned, jnp.concatenate(slope_all, 0), ((1,), (0,)))
                for q in range(2):
                    piece = slice(128 * q, 128 * q + 128)
                    out[:, lanes_at(at + 128 * q)] = blended[:, piece].T.astype(BF16)
                    turned_out[:, lanes_at(at + 128 * q)] = turned[:, piece].T.astype(BF16)
            dks.append(dk)
            dvs.append(dv)
        own_k[:, lanes_at(p * 128)] = join_sides(dks, lo) * 0.125
        own_v[:, lanes_at(p * 128)] = join_sides(dvs, lo)
        return carry

    lax.fori_loop(0, PAIRS // 2, after, 0)
    total = give[rows_of(head), :].astype(F32)
    for t, copy in d_copies:
        copy.wait_recv()
        total = total + d_buf[t].astype(F32)
    slices = total[:, : 2 * KV]
    e_copies = []
    for s, who in earlier:
        e_send[s - 1] = jnp.where(tok - owner == s, slices, 0.0).astype(BF16)
        e_copies.append(ship(e_send.at[s - 1], e_recv.at[s - 1], e_sems, s - 1, who))
    sink_sum = total[:8, 2 * KV :] + total[8:, 2 * KV :]
    z_send[...] = sink_sum
    z_copies = [(t, ship(z_send, z_recv.at[t], z_sems, t, who)) for t, who in z_peers]
    for p in range(PAIRS // 2):
        for store in stores(p):
            store.start()
    lax.fori_loop(PAIRS // 2, PAIRS, after, 0)
    for copy in e_copies:
        copy.wait_recv()
    places = [tail_of(wrap(tok + s, RING), start, parent)[1] for s in range(1, LAG + 1)]
    arrived = [e_recv[s].astype(F32) for s in range(LAG)]

    def landed(place_):
        landing = jnp.zeros((ROWS, 2 * KV), F32)
        for s in range(LAG):
            landing = landing + jnp.where(places[s] == place_, arrived[s], 0.0)
        return landing.astype(BF16)

    f_copies = []
    for t, who in peers:
        f_send[t] = landed(who[1])
        f_copies.append(ship(f_send.at[t], f_recv.at[rows_of(head)], f_sems, t, who))
    f_recv[rows_of(head), :] = landed(head)
    for p in range(PAIRS // 2, PAIRS):
        for store in stores(p):
            store.start()
    for t, copy in z_copies:
        copy.wait_recv()
        sink_sum = sink_sum + z_recv[t]
    x_send[...] = sink_sum
    x_copies = [(t, ship(x_send, x_recv.at[t], x_sems, t, who)) for t, who in x_peers]
    back_copy.wait_recv()
    own_k[...] = own_k[...] + near_back[:, :KV].astype(F32)
    own_v[...] = own_v[...] + near_back[:, KV:].astype(F32)
    for copy in f_copies:
        copy.wait_recv()
    key_grad[...] = (own_k[...] + f_recv[:, :KV].astype(F32)).astype(BF16)
    value_grad[...] = (own_v[...] + f_recv[:, KV:].astype(F32)).astype(BF16)
    for t, copy in x_copies:
        copy.wait_recv()
        sink_sum = sink_sum + x_recv[t]
    sums = jnp.sum(sink_sum, axis=1, keepdims=True)
    line = jnp.sum(jnp.where(row == lane, sums, 0.0), axis=0)
    sink_grad[...] = -line[:8]
    for copy in sent:
        copy.wait_send()
    for p in range(PAIRS):
        for store in stores(p):
            store.wait()


SMEM = pl.BlockSpec(memory_space=pltpu.SMEM)
VMEM = pl.BlockSpec(memory_space=pltpu.VMEM)
ANY = pl.BlockSpec(memory_space=pl.ANY)
DMA = pltpu.SemaphoreType.DMA


def local(queries, key_states, value_states, out_grad, sink_logits, branch_start, branch_len, parent_list):
    block = pltpu.VMEM((WINDOW, 2 * KV), BF16)
    more = 2 * KV + 128
    three = pltpu.VMEM((LAG, ROWS, 2 * KV), BF16)
    rows = pltpu.VMEM((WINDOW, 4096), BF16)
    units = (PAIRS, 8, WINDOW, 256)
    return pl.pallas_call(
        kernel,
        name="banded",
        out_shape=(
            jax.ShapeDtypeStruct((WINDOW, 4096), BF16),
            jax.ShapeDtypeStruct((WINDOW, 4096), BF16),
            jax.ShapeDtypeStruct((WINDOW, KV), BF16),
            jax.ShapeDtypeStruct((WINDOW, KV), BF16),
            jax.ShapeDtypeStruct((8,), F32),
        ),
        in_specs=[SMEM] * 4 + [ANY] * 4,
        out_specs=(ANY, ANY, VMEM, VMEM, VMEM),
        scratch_shapes=[
            rows, rows, rows, rows,
            pltpu.VMEM((WINDOW, more), BF16),
            pltpu.VMEM((GROUP, ROWS, more), BF16),
            block,
            three, three,
            pltpu.VMEM((ROWS, 2 * KV), BF16),
            block, block,
            pltpu.VMEM((GROUP, 8, 128), F32),
            pltpu.VMEM(units, F32), pltpu.VMEM(units, F32),
            pltpu.VMEM(units, BF16), pltpu.VMEM(units, BF16),
            pltpu.VMEM((WINDOW, KV), F32), pltpu.VMEM((WINDOW, KV), F32),
            pltpu.VMEM((WINDOW, more), BF16),
            pltpu.VMEM((GROUP, ROWS, more), BF16),
            block, block,
            three, three,
            pltpu.VMEM((GROUP, ROWS, 2 * KV), BF16),
            block,
            pltpu.VMEM((8, 128), F32), pltpu.VMEM((Z, 8, 128), F32),
            pltpu.VMEM((8, 128), F32), pltpu.VMEM((X, 8, 128), F32),
            pltpu.VMEM((GROUP, 8, 128), F32),
            DMA((4,)), DMA((2, PAIRS)),
            DMA((2, GROUP)), DMA((2, 2)), DMA((2, LAG)), DMA((2, GROUP)),
            DMA((2, GROUP)), DMA((2, LAG)), DMA((2, GROUP)), DMA((2, Z)), DMA((2, X)),
        ],
        compiler_params=pltpu.CompilerParams(
            collective_id=0, has_side_effects=True, vmem_limit_bytes=56 * 1024 * 1024
        ),
    )(branch_start, branch_len, parent_list.T, sink_logits, queries, out_grad, key_states, value_states)


def solution(mesh):
    rows = P(("tok", "head"), None)
    return jax.shard_map(
        local,
        mesh=mesh,
        in_specs=(rows, rows, rows, rows, P("head"), P(), P(), P()),
        out_specs=(rows, rows, rows, rows, P("head")),
        check_vma=False,
    )
```

time: 81.2 us -> 59 us (0.73); the launches traced: 79.7 us -> 58.8 us
  Pallas kernels: 66.7 us -> 52.6 us
  local copies, waits for them, and re-layouts: 12.3 us -> 5.52 us
    pallas_call x3 -> x1, Pallas kernels: 66.7 us -> 52.6 us  [local(): pl.pallas_call(kernel, name='banded', out_shape=(jax.ShapeDtypeStruct((WI...]
    unnamed x36 -> x13, local copies, waits for them, and re-layouts: 12.3 us -> 5.52 us
where the time goes in v2:
time: 59 us; the launch traced here: 58.8 us
  Pallas kernels  52.6 us (89%)
  local copies, waits for them, and re-layouts  5.52 us (9%)
  between operations  0.66 us (1%)
    pallas_call x1, Pallas kernels, local(): pl.pallas_call(kernel, name='banded', out_shape=(jax.ShapeDtypeStruct((WI...  52.6 us
    unnamed x13, local copies, waits for them, and re-layouts  5.52 us

profile of v2, /device:TPU:1, one launch (start us, length us, event | category | flops | bytes accessed | tf_op | source)
XLA Modules:
  0.0 58.8 jit_solution(5511285550243266597)
XLA Ops:
  0.6 52.6 %banded.1 = (bf16[128,4096]{1,0:T(8,128)(2,1)}, bf16[128,4096]{1,0:T(8,128)(2,1)}, bf16[128,512]{1,0:T(8,128)(2,1)}, bf16[128,512]{1,0:T(8,128)(2,1)}, f32[8]{0:T(128)}) custom-call(s32[64]{0:T(128)} %start.1, s32[64]{0:T(128)} %length.1, s32[2,64]{1,0:T(2,128)} %bitcast.1, f32[8]{0:T(128)} %sink.1, bf16[128,4096]{1,0:T(8,128)(2,1)} %queries.1, ...), custom_call_target="tpu_custom_call" | custom-call | tf_op jit(solution)/shard_map/banded/pallas_call | solution.py:369
  53.2 0.0 copy-start
  53.2 2.4 %copy.18 = bf16[128,4096]{1,0:T(8,128)(2,1)} copy(bf16[128,4096]{1,0:T(8,128)(2,1)} %get-tuple-element.10) | data formatting | bytes 2097152
  55.6 0.0 copy-done
  55.6 0.0 copy-start.2
  55.6 1.0 %copy.19 = bf16[128,4096]{1,0:T(8,128)(2,1)} copy(bf16[128,4096]{1,0:T(8,128)(2,1)S(1)} %copy-done) | data formatting | bytes 2097152
  56.6 0.1 copy-done.2
  56.6 0.0 copy-start.1
  56.6 0.7 %copy.20 = bf16[128,512]{1,0:T(8,128)(2,1)} copy(bf16[128,512]{1,0:T(8,128)(2,1)S(1)} %copy-done.2) | data formatting | bytes 262144
  57.3 0.3 copy-done.1
  57.6 0.0 copy-start.3
  57.6 0.7 %copy.21 = bf16[128,512]{1,0:T(8,128)(2,1)} copy(bf16[128,512]{1,0:T(8,128)(2,1)S(1)} %copy-done.1) | data formatting | bytes 262144
  58.3 0.0 copy-done.3
  58.3 0.5 copy.22
Async XLA Ops:
  53.2 2.4 %copy-start = (bf16[128,4096]{1,0:T(8,128)(2,1)S(1)}, bf16[128,4096]{1,0:T(8,128)(2,1)}, u32[]{:S(2)}) copy-start(bf16[128,4096]{1,0:T(8,128)(2,1)} %get-tuple-element.11) | copy-start | bytes 3145732
  55.6 1.0 %copy-start.2 = (bf16[128,512]{1,0:T(8,128)(2,1)S(1)}, bf16[128,512]{1,0:T(8,128)(2,1)}, u32[]{:S(2)}) copy-start(bf16[128,512]{1,0:T(8,128)(2,1)} %get-tuple-element.12) | copy-start | bytes 393220
  56.6 1.0 %copy-start.1 = (bf16[128,512]{1,0:T(8,128)(2,1)S(1)}, bf16[128,512]{1,0:T(8,128)(2,1)}, u32[]{:S(2)}) copy-start(bf16[128,512]{1,0:T(8,128)(2,1)} %get-tuple-element.13) | copy-start | bytes 393220
  57.6 0.7 %copy-start.3 = (f32[8]{0:T(128)S(1)}, f32[8]{0:T(128)}, u32[]{:S(2)}) copy-start(f32[8]{0:T(128)} %get-tuple-element.14) | copy-start | bytes 100

commit v3 on v2

--- a/solution.py
+++ b/solution.py
@@ -88,10 +88,10 @@
 def kernel(
     start, length, parent, sink, queries, out_grad, keys, values,
     attn_out, query_grad, key_grad, value_grad, sink_grad,
-    query, grad, out, turned_out, pair, a_buf, near, b_send, b_recv, mine, tail, prev, table,
+    query, grad, pair, a_buf, near, b_send, b_recv, mine, tail, prev, table,
     s_own, p_own, probs, slopes, own_k, own_v,
     give, d_buf, near_send, near_back, e_send, e_recv, f_send, f_recv, z_send, z_recv, x_send, x_recv, part,
-    load_sems, store_sems, a_sems, n_sems, b_sems, c_sems, d_sems, e_sems, f_sems, z_sems, x_sems,
+    load_sems, a_sems, n_sems, b_sems, c_sems, d_sems, e_sems, f_sems, z_sems, x_sems,
 ):
     tok, head = place()
     x, z = tok // Z, lax.rem(tok, Z)
@@ -250,13 +250,6 @@
     d_copies = [(t, ship(give.at[rows_of(who[1])], d_buf.at[t], d_sems, t, who)) for t, who in peers]
     back_copy = ship(near_send, near_back, n_sems, 1, left)
 
-    def stores(p):
-        wide = lanes_at(p * 1024, 1024)
-        return (
-            pltpu.make_async_copy(out.at[:, wide], attn_out.at[:, wide], store_sems.at[0, p]),
-            pltpu.make_async_copy(turned_out.at[:, wide], query_grad.at[:, wide], store_sems.at[1, p]),
-        )
-
     def after(p, carry):
         k_own, v_own = sides(pair, p, 0.125)
         k_prev, v_prev = sides(prev, p, 0.125)
@@ -285,8 +278,8 @@
                 turned = dot(k_turned, jnp.concatenate(slope_all, 0), ((1,), (0,)))
                 for q in range(2):
                     piece = slice(128 * q, 128 * q + 128)
-                    out[:, lanes_at(at + 128 * q)] = blended[:, piece].T.astype(BF16)
-                    turned_out[:, lanes_at(at + 128 * q)] = turned[:, piece].T.astype(BF16)
+                    attn_out[:, lanes_at(at + 128 * q)] = blended[:, piece].T.astype(BF16)
+                    query_grad[:, lanes_at(at + 128 * q)] = turned[:, piece].T.astype(BF16)
             dks.append(dk)
             dvs.append(dv)
         own_k[:, lanes_at(p * 128)] = join_sides(dks, lo) * 0.125
@@ -306,9 +299,6 @@
     sink_sum = total[:8, 2 * KV :] + total[8:, 2 * KV :]
     z_send[...] = sink_sum
     z_copies = [(t, ship(z_send, z_recv.at[t], z_sems, t, who)) for t, who in z_peers]
-    for p in range(PAIRS // 2):
-        for store in stores(p):
-            store.start()
     lax.fori_loop(PAIRS // 2, PAIRS, after, 0)
     for copy in e_copies:
         copy.wait_recv()
@@ -326,9 +316,6 @@
         f_send[t] = landed(who[1])
         f_copies.append(ship(f_send.at[t], f_recv.at[rows_of(head)], f_sems, t, who))
     f_recv[rows_of(head), :] = landed(head)
-    for p in range(PAIRS // 2, PAIRS):
-        for store in stores(p):
-            store.start()
     for t, copy in z_copies:
         copy.wait_recv()
         sink_sum = sink_sum + z_recv[t]
@@ -349,14 +336,26 @@
     sink_grad[...] = -line[:8]
     for copy in sent:
         copy.wait_send()
-    for p in range(PAIRS):
-        for store in stores(p):
-            store.wait()
-
-
+
+
+def deliver(*refs):
+    copies = [pltpu.make_async_copy(refs[n], refs[5 + n], refs[10].at[n]) for n in range(5)]
+    for copy in copies:
+        copy.start()
+    for copy in copies:
+        copy.wait()
+
+
+RESULTS = (
+    ((WINDOW, 4096), BF16),
+    ((WINDOW, 4096), BF16),
+    ((WINDOW, KV), BF16),
+    ((WINDOW, KV), BF16),
+    ((8,), F32),
+)
 SMEM = pl.BlockSpec(memory_space=pltpu.SMEM)
 VMEM = pl.BlockSpec(memory_space=pltpu.VMEM)
-ANY = pl.BlockSpec(memory_space=pl.ANY)
+HBM = pl.BlockSpec(memory_space=pltpu.HBM)
 DMA = pltpu.SemaphoreType.DMA
 
 
@@ -366,20 +365,14 @@
     three = pltpu.VMEM((LAG, ROWS, 2 * KV), BF16)
     rows = pltpu.VMEM((WINDOW, 4096), BF16)
     units = (PAIRS, 8, WINDOW, 256)
-    return pl.pallas_call(
+    results = pl.pallas_call(
         kernel,
         name="banded",
-        out_shape=(
-            jax.ShapeDtypeStruct((WINDOW, 4096), BF16),
-            jax.ShapeDtypeStruct((WINDOW, 4096), BF16),
-            jax.ShapeDtypeStruct((WINDOW, KV), BF16),
-            jax.ShapeDtypeStruct((WINDOW, KV), BF16),
-            jax.ShapeDtypeStruct((8,), F32),
-        ),
-        in_specs=[SMEM] * 4 + [ANY] * 4,
-        out_specs=(ANY, ANY, VMEM, VMEM, VMEM),
+        out_shape=tuple(pltpu.VMEM(shape, kind) for shape, kind in RESULTS),
+        in_specs=[SMEM] * 4 + [HBM] * 4,
+        out_specs=(VMEM,) * 5,
         scratch_shapes=[
-            rows, rows, rows, rows,
+            rows, rows,
             pltpu.VMEM((WINDOW, more), BF16),
             pltpu.VMEM((GROUP, ROWS, more), BF16),
             block,
@@ -399,14 +392,28 @@
             pltpu.VMEM((8, 128), F32), pltpu.VMEM((Z, 8, 128), F32),
             pltpu.VMEM((8, 128), F32), pltpu.VMEM((X, 8, 128), F32),
             pltpu.VMEM((GROUP, 8, 128), F32),
-            DMA((4,)), DMA((2, PAIRS)),
+            DMA((4,)),
             DMA((2, GROUP)), DMA((2, 2)), DMA((2, LAG)), DMA((2, GROUP)),
             DMA((2, GROUP)), DMA((2, LAG)), DMA((2, GROUP)), DMA((2, Z)), DMA((2, X)),
         ],
         compiler_params=pltpu.CompilerParams(
-            collective_id=0, has_side_effects=True, vmem_limit_bytes=56 * 1024 * 1024
+            collective_id=0, has_side_effects=True, vmem_limit_bytes=58 * 1024 * 1024
         ),
-    )(branch_start, branch_len, parent_list.T, sink_logits, queries, out_grad, key_states, value_states)
+    )(
+        branch_start,
+        branch_len,
+        parent_list.T,
+        sink_logits,
+        *(pltpu.with_memory_space_constraint(x, pltpu.HBM) for x in (queries, out_grad, key_states, value_states)),
+    )
+    return pl.pallas_call(
+        deliver,
+        name="deliver",
+        out_shape=tuple(jax.ShapeDtypeStruct(shape, kind) for shape, kind in RESULTS),
+        in_specs=[VMEM] * 5,
+        out_specs=(HBM,) * 5,
+        scratch_shapes=[DMA((5,))],
+    )(*(pltpu.with_memory_space_constraint(result, pltpu.VMEM) for result in results))
 
 
 def solution(mesh):

time: 59 us -> 54 us (0.915)
  local copies, waits for them, and re-layouts: 5.52 us -> 0 us
  Pallas kernels: 52.6 us -> 53.2 us
    unnamed x13 -> x0, local copies, waits for them, and re-layouts: 5.52 us -> none
    pallas_call x1 -> x2, Pallas kernels: 52.6 us -> 53.2 us  [the longest x1 51.8 us: local(): pl.pallas_call(kernel, name='banded', out_shape=tuple((pltpu.VMEM(shape,...]
where the time goes in v3:
time: 54 us; the launch traced here: 53.9 us
  Pallas kernels  53.2 us (99%)
  between operations  0.64 us (1%)
    pallas_call x1, Pallas kernels, local(): pl.pallas_call(kernel, name='banded', out_shape=tuple((pltpu.VMEM(shape,...  51.8 us
    pallas_call x1, Pallas kernels, local(): pl.pallas_call(deliver, name='deliver', out_shape=tuple((jax.ShapeDtypeSt...  1.44 us

profile of v3, /device:TPU:1, one launch (start us, length us, event | category | flops | bytes accessed | tf_op | source)
XLA Modules:
  0.0 53.9 jit_solution(9818881586310419005)
XLA Ops:
  0.6 51.8 %banded.1 = (bf16[128,4096]{1,0:T(8,128)(2,1)S(1)}, bf16[128,4096]{1,0:T(8,128)(2,1)S(1)}, bf16[128,512]{1,0:T(8,128)(2,1)S(1)}, bf16[128,512]{1,0:T(8,128)(2,1)S(1)}, f32[8]{0:T(128)S(1)}) custom-call(s32[64]{0:T(128)} %start.1, s32[64]{0:T(128)} %length.1, s32[2,64]{1,0:T(2,128)} %bitcast.1, f32[8]{0:T(128)} %sink.1, bf16[128,4096]{1,0:T(8,128)(2,1)} %queries.1, ...), custom_call_target="tpu_custom_call" | custom-call | tf_op jit(solution)/shard_map/banded/pallas_call | solution.py:368
  52.4 1.4 %deliver.1 = (bf16[128,4096]{1,0:T(8,128)(2,1)}, bf16[128,4096]{1,0:T(8,128)(2,1)}, bf16[128,512]{1,0:T(8,128)(2,1)}, bf16[128,512]{1,0:T(8,128)(2,1)}, f32[8]{0:T(128)}) custom-call(bf16[128,4096]{1,0:T(8,128)(2,1)S(1)} %get-tuple-element.10.refs_0_, bf16[128,4096]{1,0:T(8,128)(2,1)S(1)} %get-tuple-element.11.refs_1_, ...), custom_call_target="tpu_custom_call" | custom-call | tf_op jit(solution)/shard_map/deliver/pallas_call | solution.py:409

commit v4 on v3

v4 whole, which is shorter than its diff:
```python
import jax
import jax.numpy as jnp
from jax import lax
from jax.experimental import pallas as pl
from jax.experimental.pallas import tpu as pltpu
from jax.sharding import PartitionSpec as P

HEAD_DIM = 64
WINDOW = 128
LAG = 3
PAIRS = 4
BR_DEV = 2
GROUP = 8
RING = 32
ROWS = WINDOW // GROUP
KV = 512
Z = 8
X = 4
F32 = jnp.float32
BF16 = jnp.bfloat16
MESH = pl.DeviceIdType.MESH


def place():
    return lax.axis_index("tok"), lax.axis_index("head")


def block_state(tok, head, start, length, parent):
    pos = (tok * GROUP + head) * WINDOW
    alive, opening = False, False
    for b in range(BR_DEV):
        first = start[tok * BR_DEV + b]
        covers = (first <= pos) & (pos < first + length[tok * BR_DEV + b])
        alive = alive | covers
        opening = opening | (covers & (first == pos))
    return alive, opening, parent[0, tok * BR_DEV] >= 0


def tail_of(tok, start, parent):
    row = tok * BR_DEV
    token = start[jnp.maximum(parent[0, row], 0)] + parent[1, row]
    return lax.shift_right_logical(token, 10), lax.shift_right_logical(token, 7) & (GROUP - 1)


def send(src, dst, sems, slot, tok, head):
    copy = pltpu.make_async_remote_copy(
        src_ref=src,
        dst_ref=dst,
        send_sem=sems.at[0, slot],
        recv_sem=sems.at[1, slot],
        device_id=(tok, head),
        device_id_type=MESH,
    )
    copy.start()
    return copy


def wrap(value, count):
    return lax.rem(value + count, count)


def dot(left, right, dims):
    return lax.dot_general(left, right, (dims, ((), ())), preferred_element_type=F32)


def both_sides(block, lo):
    turned = pltpu.roll(block, HEAD_DIM, 1)
    zero = jnp.zeros_like(block)
    return (
        (jnp.where(lo, block, zero), jnp.where(lo, zero, turned)),
        (jnp.where(lo, turned, zero), jnp.where(lo, zero, block)),
    )


def join_sides(parts, lo):
    (a0, a1), (b0, b1) = parts
    return jnp.where(lo, a0, b1) + pltpu.roll(jnp.where(lo, b0, a1), HEAD_DIM, 1)


FAR_FIRST = (4, 5, 3, 6, 2, 7, 1)


def split_rows(rows):
    high = rows.astype(BF16).astype(F32)
    return jnp.concatenate([high, rows - high], 1).astype(BF16)


def kernel(
    start_in, length_in, parent_in, sink_in, queries, out_grad, keys, values,
    attn_out, query_grad, key_grad, value_grad, sink_grad,
    start, length, parent, sink, query, grad, pair, ak_buf, av_buf, near, b_send, bk_recv, bv_recv, mine, tail, prev, table,
    q_turned, g_turned, s_own, p_own, probs, slopes, own_k, own_v,
    give, dv_buf, dk_buf, near_send, near_back, e_send, e_recv, f_send, f_recv, z_send, z_recv, x_send, x_recv, part, lines,
    load_sems, a_sems, n_sems, b_sems, c_sems, d_sems, e_sems, f_sems, z_sems, x_sems,
):
    tok, head = place()
    x, z = tok // Z, lax.rem(tok, Z)
    peers = [(t, (tok, wrap(head + t, GROUP))) for t in FAR_FIRST]
    later = [(s, (wrap(tok + s, RING), head)) for s in (3, 2, 1)]
    earlier = [(s, (wrap(tok - s, RING), head)) for s in (3, 2, 1)]
    z_peers = [(t, (x * Z + wrap(z + t, Z), head)) for t in FAR_FIRST]
    x_peers = [(t, (wrap(x + t, X) * Z + z, head)) for t in (2, 3, 1)]
    right, left = (tok, wrap(head + 1, GROUP)), (tok, wrap(head - 1, GROUP))

    loads = [
        pltpu.make_async_copy(src, dst, load_sems.at[n])
        for n, (src, dst) in enumerate((
            (keys, pair.at[:, pl.ds(0, KV)]), (values, pair.at[:, pl.ds(KV, KV)]), (sink_in, sink), (start_in, start),
            (length_in, length), (parent_in, parent), (queries, query), (out_grad, grad),
        ))
    ]
    for load in loads:
        load.start()
    barrier = pltpu.get_barrier_semaphore()
    partners = [who for _, who in z_peers + later + earlier + peers + x_peers]
    for who in partners:
        pl.semaphore_signal(barrier, inc=1, device_id=who, device_id_type=MESH)

    for load in loads[2:6]:
        load.wait()
    alive, opening, rooted = block_state(tok, head, start, length, parent)
    ok = alive & (jnp.logical_not(opening) | rooted)
    outward = opening & rooted
    inward = alive & jnp.logical_not(opening)
    row = lax.broadcasted_iota(jnp.int32, (8, 128), 0)
    lane = lax.broadcasted_iota(jnp.int32, (8, 128), 1)
    sink_tile = jnp.zeros((8, 128), F32)
    for g in range(8):
        sink_tile = jnp.where(row == g, sink[g], sink_tile)
    table[head] = sink_tile
    pair[:, 2 * KV :] = split_rows(jnp.broadcast_to(sink_tile[None], (GROUP, 8, 128))).reshape(WINDOW, 128)
    loads[0].wait()
    loads[1].wait()
    pl.semaphore_wait(barrier, len(partners))

    def rows_of(place_):
        return pl.ds(pl.multiple_of(place_ * ROWS, ROWS), ROWS)

    sent = []

    def ship(src, dst, sems, slot, who):
        copy = send(src, dst, sems, slot, *who)
        sent.append(copy)
        return copy

    keys_at, values_at = pl.ds(0, KV), pl.ds(KV, KV)
    ak_copies = [ship(pair.at[rows_of(who[1]), keys_at], ak_buf.at[t], a_sems, t, who) for t, who in peers]
    av_copies = [
        ship(pair.at[rows_of(who[1]), pl.ds(KV, KV + 128)], av_buf.at[t], a_sems, GROUP + t, who) for t, who in peers
    ]
    ak_buf[0] = pair[rows_of(head), :KV]
    av_buf[0] = pair[rows_of(head), KV:]

    lo = lax.broadcasted_iota(jnp.int32, (WINDOW, 128), 1) < HEAD_DIM
    place_j = lax.broadcasted_iota(jnp.int32, (WINDOW, 256), 0)
    place_i = lax.broadcasted_iota(jnp.int32, (WINDOW, 256), 1) & (WINDOW - 1)
    causal = place_j <= place_i
    causal16 = causal.astype(F32).astype(BF16)
    bias = jnp.where(ok, 0.0, -jnp.inf)

    def lanes_at(at, size=128):
        return pl.ds(pl.multiple_of(at, size), size)

    def sides(ref, p, factor):
        k = both_sides(ref[:, lanes_at(p * 128)].astype(F32) * factor, lo)
        v = both_sides(ref[:, lanes_at(KV + p * 128)].astype(F32), lo)
        return k, v

    def stacked(ref, at):
        return jnp.concatenate([ref[:, lanes_at(at)], ref[:, lanes_at(at + 128)]], 0)

    def both_rows(sides_):
        return jnp.concatenate([side.astype(BF16) for side in sides_], 0)

    def before(p, carry):
        wide = lanes_at(p * 1024, 1024)
        grad[:, wide] = jnp.where(alive, grad[:, wide], jnp.zeros((), BF16))
        k, v = sides(pair, p, 0.125)
        for c in range(2):
            k_rows, v_rows = both_rows(k[c]), both_rows(v[c])
            for half in range(2):
                at = p * 1024 + 512 * c + 256 * half
                for ref, turned_ref, rows, own in (
                    (query, q_turned, k_rows, s_own), (grad, g_turned, v_rows, p_own)
                ):
                    turned = jnp.concatenate([ref[:, lanes_at(at + 128 * q)].T for q in range(2)], 1)
                    turned_ref[p, 2 * c + half] = turned
                    own[p, 2 * c + half] = dot(rows, turned, ((1,), (0,)))
        return carry

    loads[6].wait()
    loads[7].wait()
    lax.fori_loop(0, PAIRS // 2, before, 0)

    tails = [(s, who, (head - tail_of(who[0], start, parent)[1]) & (GROUP - 1)) for s, who in later]

    def pass_on(a_buf, b_recv, chunk):
        copies = []
        for s, who, slot in tails:
            b_send[chunk, s - 1] = a_buf[slot][:, :KV]
            copies.append(ship(b_send.at[chunk, s - 1], b_recv.at[s - 1], b_sems, LAG * chunk + s - 1, who))
        return copies

    for copy in ak_copies:
        copy.wait_recv()
    bk_copies = pass_on(ak_buf, bk_recv, 0)
    for copy in av_copies:
        copy.wait_recv()
    bv_copies = pass_on(av_buf, bv_recv, 1)
    near_copies = [
        ship(pair.at[:, at], near.at[:, at], n_sems, n, right) for n, at in enumerate((keys_at, values_at))
    ]
    for t in range(1, GROUP):
        extra = av_buf[t, :, KV:].astype(F32)
        table[wrap(head - t, GROUP)] = extra[:8] + extra[8:]
    for h in range(GROUP):
        for line in range(4):
            first = 4 * (line // 2) + line % 2
            both = [table[h, first + 2 * q : first + 2 * q + 1, :] for q in range(2)]
            at = 4 * (h % 2) + line
            lines[h // 2, at : at + 1, :] = jnp.concatenate(both, 1)
    lax.fori_loop(PAIRS // 2, PAIRS, before, 0)
    owner, _ = tail_of(tok, start, parent)
    behind = jnp.clip(tok - owner - 1, 0, LAG - 1)

    def spread(copies, b_recv, chunk, at):
        for copy in copies:
            copy.wait_recv()
        mine[chunk] = b_recv[behind]
        tail[rows_of(head), at] = mine[chunk]
        return [
            ship(mine.at[chunk], tail.at[rows_of(head), at], c_sems, GROUP * chunk + t, who) for t, who in peers
        ]

    ck_copies = spread(bk_copies, bk_recv, 0, keys_at)
    cv_copies = spread(bv_copies, bv_recv, 1, values_at)

    def choose(copies, near_copy, at):
        near_copy.wait_recv()
        for copy in copies:
            copy.wait_recv()
        prev[:, at] = jnp.where(ok, jnp.where(opening, tail[:, at], near[:, at]), jnp.zeros((), BF16))

    choose(ck_copies, near_copies[0], keys_at)

    zero16 = jnp.zeros((), BF16)

    def hand(p, block, give_at, near_at):
        block = block.astype(BF16)
        give[:, lanes_at(give_at + p * 128)] = jnp.where(outward, block, zero16)
        near_send[:, lanes_at(near_at + p * 128)] = jnp.where(inward, block, zero16)

    def weigh(p, carry):
        k = both_sides(prev[:, lanes_at(p * 128)].astype(F32) * 0.125, lo)
        dvs = []
        for c in range(2):
            k_rows = both_rows(k[c])
            dv = jnp.zeros((256, 128), F32)
            for half in range(2):
                unit = 2 * c + half
                g_rows = stacked(grad, p * 1024 + 512 * c + 256 * half)
                scores_both = dot(k_rows, q_turned[p, unit], ((1,), (0,)))
                behind16 = []
                for e in range(2):
                    at, line = slice(128 * e, 128 * e + 128), 2 * unit + e
                    scores = jnp.where(causal, s_own[p, unit, at], scores_both[at] + bias)
                    sinks = lines[p, line : line + 1, :]
                    peak = jnp.maximum(jnp.max(scores, axis=0, keepdims=True), sinks)
                    exps = jnp.exp(scores - peak)
                    sink_exp = jnp.exp(sinks - peak)
                    inverse = 1.0 / (jnp.sum(exps, axis=0, keepdims=True) + sink_exp)
                    prob = exps * inverse
                    s_own[p, unit, at] = prob
                    part[p, line : line + 1, :] = sink_exp * inverse
                    prob16 = prob.astype(BF16)
                    probs[p, unit, at] = prob16
                    behind16.append(prob16 - prob16 * causal16)
                dv = dv + dot(jnp.concatenate(behind16, 0), g_rows, ((1,), (0,)))
            dvs.append((dv[:WINDOW], dv[WINDOW:]))
        hand(p, join_sides(dvs, lo), 0, KV)
        return carry

    lax.fori_loop(0, PAIRS, weigh, 0)
    dv_copies = [ship(give.at[rows_of(who[1]), pl.ds(0, KV)], dv_buf.at[t], d_sems, t, who) for t, who in peers]
    back_copies = [ship(near_send.at[:, values_at], near_back.at[:, values_at], n_sems, 2, left)]
    choose(cv_copies, near_copies[1], values_at)

    def incline(p, carry):
        v = both_sides(prev[:, lanes_at(KV + p * 128)].astype(F32), lo)
        dks = []
        for c in range(2):
            v_rows = both_rows(v[c])
            dk = jnp.zeros((256, 128), F32)
            for half in range(2):
                unit = 2 * c + half
                q_rows = stacked(query, p * 1024 + 512 * c + 256 * half)
                inner_both = dot(v_rows, g_turned[p, unit], ((1,), (0,)))
                behind16 = []
                for e in range(2):
                    at, line = slice(128 * e, 128 * e + 128), 2 * unit + e
                    inner = jnp.where(causal, p_own[p, unit, at], inner_both[at])
                    prob = s_own[p, unit, at]
                    weighed = prob * inner
                    delta = jnp.sum(weighed, axis=0, keepdims=True)
                    slope16 = (weighed - prob * delta).astype(BF16)
                    part[p, line : line + 1, :] = part[p, line : line + 1, :] * delta
                    slopes[p, unit, at] = slope16
                    behind16.append(slope16 - slope16 * causal16)
                dk = dk + dot(jnp.concatenate(behind16, 0), q_rows, ((1,), (0,)))
            dks.append((dk[:WINDOW], dk[WINDOW:]))
        hand(p, join_sides(dks, lo) * 0.125, KV, 0)
        return carry

    lax.fori_loop(0, PAIRS, incline, 0)
    terms = part[...].reshape(GROUP, 4, 256)
    terms = jnp.concatenate([terms[:, :, :128], terms[:, :, 128:]], 1)
    give[:, 2 * KV :] = split_rows(terms).reshape(WINDOW, 128)
    dk_copies = [
        ship(give.at[rows_of(who[1]), pl.ds(KV, KV + 128)], dk_buf.at[t], d_sems, GROUP + t, who) for t, who in peers
    ]

    def after(p, carry):
        k_own, v_own = sides(pair, p, 0.125)
        k_prev, v_prev = sides(prev, p, 0.125)
        dks, dvs = [], []
        for c in range(2):
            k_all = jnp.concatenate([k_own[c][0], k_prev[c][0], k_own[c][1], k_prev[c][1]], 0)
            v_all = jnp.concatenate([v_own[c][0], v_prev[c][0], v_own[c][1], v_prev[c][1]], 0)
            k_turned = k_all.T.astype(BF16)
            v_turned = v_all.T.astype(BF16)
            dk, dv = jnp.zeros((256, 128), F32), jnp.zeros((256, 128), F32)
            for half in range(2):
                at, unit = p * 1024 + 512 * c + 256 * half, 2 * c + half
                q_rows, g_rows = stacked(query, at), stacked(grad, at)
                prob_all, slope_all, prob_own, slope_own = [], [], [], []
                for e in range(2):
                    prob16 = probs[p, unit, 128 * e : 128 * e + 128]
                    slope16 = slopes[p, unit, 128 * e : 128 * e + 128]
                    prob_own.append(prob16 * causal16)
                    slope_own.append(slope16 * causal16)
                    prob_all += [prob_own[e], prob16 - prob_own[e]]
                    slope_all += [slope_own[e], slope16 - slope_own[e]]
                dk = dk + dot(jnp.concatenate(slope_own, 0), q_rows, ((1,), (0,)))
                dv = dv + dot(jnp.concatenate(prob_own, 0), g_rows, ((1,), (0,)))
                blended = dot(v_turned, jnp.concatenate(prob_all, 0), ((1,), (0,)))
                blended = jnp.where(alive, blended, 0.0)
                turned = dot(k_turned, jnp.concatenate(slope_all, 0), ((1,), (0,)))
                for q in range(2):
                    piece = slice(128 * q, 128 * q + 128)
                    attn_out[:, lanes_at(at + 128 * q)] = blended[:, piece].T.astype(BF16)
                    query_grad[:, lanes_at(at + 128 * q)] = turned[:, piece].T.astype(BF16)
            dks.append((dk[:WINDOW], dk[WINDOW:]))
            dvs.append((dv[:WINDOW], dv[WINDOW:]))
        own_k[:, lanes_at(p * 128)] = join_sides(dks, lo) * 0.125
        own_v[:, lanes_at(p * 128)] = join_sides(dvs, lo)
        return carry

    def gather(copies, own, d_buf):
        total = own.astype(F32)
        for (t, _), copy in zip(peers, copies):
            copy.wait_recv()
            total = total + d_buf[t].astype(F32)
        return total

    def send_back(slices, chunk):
        copies = []
        for s, who in earlier:
            e_send[chunk, s - 1] = jnp.where(tok - owner == s, slices, 0.0).astype(BF16)
            copies.append(ship(e_send.at[chunk, s - 1], e_recv.at[chunk, s - 1], e_sems, LAG * chunk + s - 1, who))
        return copies

    ev_copies = send_back(gather(dv_copies, give[rows_of(head), :KV], dv_buf), 1)
    lax.fori_loop(0, 1, after, 0)
    total = gather(dk_copies, give[rows_of(head), KV:], dk_buf)
    ek_copies = send_back(total[:, :KV], 0)
    sink_sum = total[:8, KV:] + total[8:, KV:]
    z_send[...] = sink_sum
    z_copies = [(t, ship(z_send, z_recv.at[t], z_sems, t, who)) for t, who in z_peers]
    back_copies.append(ship(near_send.at[:, keys_at], near_back.at[:, keys_at], n_sems, 3, left))
    lax.fori_loop(1, 3, after, 0)
    places = [tail_of(wrap(tok + s, RING), start, parent)[1] for s in range(1, LAG + 1)]

    def land(copies, chunk, at):
        for copy in copies:
            copy.wait_recv()
        arrived = [e_recv[chunk, s].astype(F32) for s in range(LAG)]

        def landed(place_):
            landing = jnp.zeros((ROWS, KV), F32)
            for s in range(LAG):
                landing = landing + jnp.where(places[s] == place_, arrived[s], 0.0)
            return landing.astype(BF16)

        copies = []
        for t, who in peers:
            f_send[chunk, t] = landed(who[1])
            copies.append(ship(f_send.at[chunk, t], f_recv.at[rows_of(head), at], f_sems, GROUP * chunk + t, who))
        f_recv[rows_of(head), at] = landed(head)
        return copies

    f_copies = land(ev_copies, 1, values_at)
    lax.fori_loop(3, PAIRS, after, 0)
    f_copies += land(ek_copies, 0, keys_at)
    for t, copy in z_copies:
        copy.wait_recv()
        sink_sum = sink_sum + z_recv[t]
    x_send[...] = sink_sum
    x_copies = [(t, ship(x_send, x_recv.at[t], x_sems, t, who)) for t, who in x_peers]
    for copy in back_copies:
        copy.wait_recv()
    own_k[...] = own_k[...] + near_back[:, :KV].astype(F32)
    own_v[...] = own_v[...] + near_back[:, KV:].astype(F32)
    for copy in f_copies:
        copy.wait_recv()
    key_grad[...] = (own_k[...] + f_recv[:, :KV].astype(F32)).astype(BF16)
    value_grad[...] = (own_v[...] + f_recv[:, KV:].astype(F32)).astype(BF16)
    for t, copy in x_copies:
        copy.wait_recv()
        sink_sum = sink_sum + x_recv[t]
    sums = jnp.sum(sink_sum, axis=1, keepdims=True)
    place_ = 4 * ((row >> 1) & 1) + 2 * (row >> 2) + (row & 1)
    line = jnp.sum(jnp.where(place_ == lane, sums, 0.0), axis=0)
    sink_grad[...] = -line[:8]
    for copy in sent:
        copy.wait_send()


def deliver(*refs):
    copies = [pltpu.make_async_copy(refs[n], refs[5 + n], refs[10].at[n]) for n in range(5)]
    for copy in copies:
        copy.start()
    for copy in copies:
        copy.wait()


RESULTS = (
    ((WINDOW, 4096), BF16),
    ((WINDOW, 4096), BF16),
    ((WINDOW, KV), BF16),
    ((WINDOW, KV), BF16),
    ((8,), F32),
)
VMEM = pl.BlockSpec(memory_space=pltpu.VMEM)
HBM = pl.BlockSpec(memory_space=pltpu.HBM)
DMA = pltpu.SemaphoreType.DMA


def local(queries, key_states, value_states, out_grad, sink_logits, branch_start, branch_len, parent_list):
    block = pltpu.VMEM((WINDOW, 2 * KV), BF16)
    slices = pltpu.VMEM((GROUP, ROWS, KV), BF16)
    slices_more = pltpu.VMEM((GROUP, ROWS, KV + 128), BF16)
    three = pltpu.VMEM((2, LAG, ROWS, KV), BF16)
    rows = pltpu.VMEM((WINDOW, 4096), BF16)
    units = (PAIRS, 4, 2 * WINDOW, 256)
    turned = pltpu.VMEM((PAIRS, 4, 128, 256), BF16)
    results = pl.pallas_call(
        kernel,
        name="banded",
        out_shape=tuple(pltpu.VMEM(shape, kind) for shape, kind in RESULTS),
        in_specs=[HBM] * 8,
        out_specs=(VMEM,) * 5,
        scratch_shapes=[
            pltpu.SMEM((64,), jnp.int32), pltpu.SMEM((64,), jnp.int32),
            pltpu.SMEM((2, 64), jnp.int32), pltpu.SMEM((8,), F32),
            rows, rows,
            pltpu.VMEM((WINDOW, 2 * KV + 128), BF16),
            slices, slices_more,
            block,
            three,
            pltpu.VMEM((LAG, ROWS, KV), BF16), pltpu.VMEM((LAG, ROWS, KV), BF16),
            pltpu.VMEM((2, ROWS, KV), BF16),
            block, block,
            pltpu.VMEM((GROUP, 8, 128), F32),
            turned, turned,
            pltpu.VMEM(units, F32), pltpu.VMEM(units, F32),
            pltpu.VMEM(units, BF16), pltpu.VMEM(units, BF16),
            pltpu.VMEM((WINDOW, KV), F32), pltpu.VMEM((WINDOW, KV), F32),
            pltpu.VMEM((WINDOW, 2 * KV + 128), BF16),
            slices, slices_more,
            block, block,
            three, three,
            pltpu.VMEM((2, GROUP, ROWS, KV), BF16),
            block,
            pltpu.VMEM((8, 128), F32), pltpu.VMEM((Z, 8, 128), F32),
            pltpu.VMEM((8, 128), F32), pltpu.VMEM((X, 8, 128), F32),
            pltpu.VMEM((PAIRS, 8, 256), F32), pltpu.VMEM((PAIRS, 8, 256), F32),
            DMA((8,)),
            DMA((2, 2 * GROUP)), DMA((2, 4)), DMA((2, 2 * LAG)), DMA((2, 2 * GROUP)),
            DMA((2, 2 * GROUP)), DMA((2, 2 * LAG)), DMA((2, 2 * GROUP)), DMA((2, Z)), DMA((2, X)),
        ],
        compiler_params=pltpu.CompilerParams(
            collective_id=0, has_side_effects=True, vmem_limit_bytes=58 * 1024 * 1024
        ),
    )(
        *(
            pltpu.with_memory_space_constraint(x, pltpu.HBM)
            for x in (
                branch_start, branch_len, parent_list.T, sink_logits, queries, out_grad, key_states, value_states
            )
        ),
    )
    return pl.pallas_call(
        deliver,
        name="deliver",
        out_shape=tuple(jax.ShapeDtypeStruct(shape, kind) for shape, kind in RESULTS),
        in_specs=[VMEM] * 5,
        out_specs=(HBM,) * 5,
        scratch_shapes=[DMA((5,))],
    )(*(pltpu.with_memory_space_constraint(result, pltpu.VMEM) for result in results))


def solution(mesh):
    rows = P(("tok", "head"), None)
    return jax.shard_map(
        local,
        mesh=mesh,
        in_specs=(rows, rows, rows, rows, P("head"), P(), P(), P()),
        out_specs=(rows, rows, rows, rows, P("head")),
        check_vma=False,
    )
```

time: 54 us -> 48 us (0.89)
  Pallas kernels: 53.2 us -> 47.2 us
    pallas_call x1, Pallas kernels: 51.8 us -> 45.8 us  [local(): pl.pallas_call(kernel, name='banded', out_shape=tuple((pltpu.VMEM(shape,...]
where the time goes in v4:
time: 48 us; the launch traced here: 47.9 us
  Pallas kernels  47.2 us (98%)
  between operations  0.64 us (1%)
    pallas_call x1, Pallas kernels, local(): pl.pallas_call(kernel, name='banded', out_shape=tuple((pltpu.VMEM(shape,...  45.8 us
    pallas_call x1, Pallas kernels, local(): pl.pallas_call(deliver, name='deliver', out_shape=tuple((jax.ShapeDtypeSt...  1.44 us

profile of v4, /device:TPU:1, one launch (start us, length us, event | category | flops | bytes accessed | tf_op | source)
XLA Modules:
  0.0 47.9 jit_solution(10793371341387368398)
XLA Ops:
  0.6 45.8 %banded.1 = (bf16[128,4096]{1,0:T(8,128)(2,1)S(1)}, bf16[128,4096]{1,0:T(8,128)(2,1)S(1)}, bf16[128,512]{1,0:T(8,128)(2,1)S(1)}, bf16[128,512]{1,0:T(8,128)(2,1)S(1)}, f32[8]{0:T(128)S(1)}) custom-call(s32[64]{0:T(128)} %start_in.1, s32[64]{0:T(128)} %length_in.1, s32[2,64]{1,0:T(2,128)} %bitcast.1, f32[8]{0:T(128)} %sink_in.1, bf16[128,4096]{1,0:T(8,128)(2,1)} %queries.1, ...), custom_call_target="tpu_custom_call" | custom-call | tf_op jit(solution)/shard_map/banded/pallas_call | solution.py:456
  46.4 1.4 %deliver.1 = (bf16[128,4096]{1,0:T(8,128)(2,1)}, bf16[128,4096]{1,0:T(8,128)(2,1)}, bf16[128,512]{1,0:T(8,128)(2,1)}, bf16[128,512]{1,0:T(8,128)(2,1)}, f32[8]{0:T(128)}) custom-call(bf16[128,4096]{1,0:T(8,128)(2,1)S(1)} %get-tuple-element.10.refs_0_, bf16[128,4096]{1,0:T(8,128)(2,1)S(1)} %get-tuple-element.11.refs_1_, ...), custom_call_target="tpu_custom_call" | custom-call | tf_op jit(solution)/shard_map/deliver/pallas_call | solution.py:502

commit v5 on v4

--- a/solution.py
+++ b/solution.py
@@ -8,6 +8,8 @@
 HEAD_DIM = 64
 WINDOW = 128
 LAG = 3
+CHUNKS = 4
+PART = 256
 PAIRS = 4
 BR_DEV = 2
 GROUP = 8
@@ -88,9 +90,9 @@
 def kernel(
     start_in, length_in, parent_in, sink_in, queries, out_grad, keys, values,
     attn_out, query_grad, key_grad, value_grad, sink_grad,
-    start, length, parent, sink, query, grad, pair, ak_buf, av_buf, near, b_send, bk_recv, bv_recv, mine, tail, prev, table,
+    start, length, parent, sink, query, grad, pair, a0, a1, a2, a3, near, b_send, b0, b1, b2, b3, mine, tail, prev, table,
     q_turned, g_turned, s_own, p_own, probs, slopes, own_k, own_v,
-    give, dv_buf, dk_buf, near_send, near_back, e_send, e_recv, f_send, f_recv, z_send, z_recv, x_send, x_recv, part, lines,
+    give, d_buf, near_send, near_back, e_send, e_recv, f_send, f_recv, z_send, z_recv, x_send, x_recv, part, lines,
     load_sems, a_sems, n_sems, b_sems, c_sems, d_sems, e_sems, f_sems, z_sems, x_sems,
 ):
     tok, head = place()
@@ -144,12 +146,20 @@
         return copy
 
     keys_at, values_at = pl.ds(0, KV), pl.ds(KV, KV)
-    ak_copies = [ship(pair.at[rows_of(who[1]), keys_at], ak_buf.at[t], a_sems, t, who) for t, who in peers]
-    av_copies = [
-        ship(pair.at[rows_of(who[1]), pl.ds(KV, KV + 128)], av_buf.at[t], a_sems, GROUP + t, who) for t, who in peers
+    a_bufs, b_recvs = (a0, a1, a2, a3), (b0, b1, b2, b3)
+
+    def chunk_at(n):
+        return pl.ds(PART * n, PART)
+
+    def wide_at(n):
+        return pl.ds(PART * n, PART + 128 if n == CHUNKS - 1 else PART)
+
+    a_copies = [
+        [ship(pair.at[rows_of(who[1]), wide_at(n)], a_bufs[n].at[t], a_sems, GROUP * n + t, who) for t, who in peers]
+        for n in range(CHUNKS)
     ]
-    ak_buf[0] = pair[rows_of(head), :KV]
-    av_buf[0] = pair[rows_of(head), KV:]
+    for n in range(CHUNKS):
+        a_bufs[n][0] = pair[rows_of(head), wide_at(n)]
 
     lo = lax.broadcasted_iota(jnp.int32, (WINDOW, 128), 1) < HEAD_DIM
     place_j = lax.broadcasted_iota(jnp.int32, (WINDOW, 256), 0)
@@ -194,24 +204,19 @@
 
     tails = [(s, who, (head - tail_of(who[0], start, parent)[1]) & (GROUP - 1)) for s, who in later]
 
-    def pass_on(a_buf, b_recv, chunk):
-        copies = []
+    b_copies = []
+    for n in range(CHUNKS):
+        for copy in a_copies[n]:
+            copy.wait_recv()
+        b_copies.append([])
         for s, who, slot in tails:
-            b_send[chunk, s - 1] = a_buf[slot][:, :KV]
-            copies.append(ship(b_send.at[chunk, s - 1], b_recv.at[s - 1], b_sems, LAG * chunk + s - 1, who))
-        return copies
-
-    for copy in ak_copies:
-        copy.wait_recv()
-    bk_copies = pass_on(ak_buf, bk_recv, 0)
-    for copy in av_copies:
-        copy.wait_recv()
-    bv_copies = pass_on(av_buf, bv_recv, 1)
+            b_send[n, s - 1] = a_bufs[n][slot][:, :PART]
+            b_copies[n].append(ship(b_send.at[n, s - 1], b_recvs[n].at[s - 1], b_sems, LAG * n + s - 1, who))
     near_copies = [
         ship(pair.at[:, at], near.at[:, at], n_sems, n, right) for n, at in enumerate((keys_at, values_at))
     ]
     for t in range(1, GROUP):
-        extra = av_buf[t, :, KV:].astype(F32)
+        extra = a3[t, :, PART:].astype(F32)
         table[wrap(head - t, GROUP)] = extra[:8] + extra[8:]
     for h in range(GROUP):
         for line in range(4):
@@ -223,25 +228,30 @@
     owner, _ = tail_of(tok, start, parent)
     behind = jnp.clip(tok - owner - 1, 0, LAG - 1)
 
-    def spread(copies, b_recv, chunk, at):
-        for copy in copies:
+    c_copies = []
+    for n in range(CHUNKS):
+        for copy in b_copies[n]:
             copy.wait_recv()
-        mine[chunk] = b_recv[behind]
-        tail[rows_of(head), at] = mine[chunk]
+        mine[n] = b_recvs[n][behind]
+        tail[rows_of(head), chunk_at(n)] = mine[n]
+        c_copies.append([
+            ship(mine.at[n], tail.at[rows_of(head), chunk_at(n)], c_sems, GROUP * n + t, who) for t, who in peers
+        ])
+
+    def choose(n):
+        if n % 2 == 0:
+            near_copies[n // 2].wait_recv()
+        for copy in c_copies[n]:
+            copy.wait_recv()
+        at = chunk_at(n)
+        prev[:, at] = jnp.where(ok, jnp.where(opening, tail[:, at], near[:, at]), jnp.zeros((), BF16))
+
+    def gather_from(n):
         return [
-            ship(mine.at[chunk], tail.at[rows_of(head), at], c_sems, GROUP * chunk + t, who) for t, who in peers
+            ship(give.at[rows_of(who[1]), wide_at(n)], d_buf.at[n, t, :, pl.ds(0, PART + 128 if n == CHUNKS - 1 else PART)],
+                 d_sems, GROUP * n + t, who)
+            for t, who in peers
         ]
-
-    ck_copies = spread(bk_copies, bk_recv, 0, keys_at)
-    cv_copies = spread(bv_copies, bv_recv, 1, values_at)
-
-    def choose(copies, near_copy, at):
-        near_copy.wait_recv()
-        for copy in copies:
-            copy.wait_recv()
-        prev[:, at] = jnp.where(ok, jnp.where(opening, tail[:, at], near[:, at]), jnp.zeros((), BF16))
-
-    choose(ck_copies, near_copies[0], keys_at)
 
     zero16 = jnp.zeros((), BF16)
 
@@ -280,10 +290,12 @@
         hand(p, join_sides(dvs, lo), 0, KV)
         return carry
 
-    lax.fori_loop(0, PAIRS, weigh, 0)
-    dv_copies = [ship(give.at[rows_of(who[1]), pl.ds(0, KV)], dv_buf.at[t], d_sems, t, who) for t, who in peers]
+    d_copies = []
+    for n in range(2):
+        choose(n)
+        lax.fori_loop(2 * n, 2 * n + 2, weigh, 0)
+        d_copies.append(gather_from(n))
     back_copies = [ship(near_send.at[:, values_at], near_back.at[:, values_at], n_sems, 2, left)]
-    choose(cv_copies, near_copies[1], values_at)
 
     def incline(p, carry):
         v = both_sides(prev[:, lanes_at(KV + p * 128)].astype(F32), lo)
@@ -311,13 +323,15 @@
         hand(p, join_sides(dks, lo) * 0.125, KV, 0)
         return carry
 
-    lax.fori_loop(0, PAIRS, incline, 0)
+    choose(2)
+    lax.fori_loop(0, 2, incline, 0)
+    d_copies.append(gather_from(2))
+    choose(3)
+    lax.fori_loop(2, PAIRS, incline, 0)
     terms = part[...].reshape(GROUP, 4, 256)
     terms = jnp.concatenate([terms[:, :, :128], terms[:, :, 128:]], 1)
     give[:, 2 * KV :] = split_rows(terms).reshape(WINDOW, 128)
-    dk_copies = [
-        ship(give.at[rows_of(who[1]), pl.ds(KV, KV + 128)], dk_buf.at[t], d_sems, GROUP + t, who) for t, who in peers
-    ]
+    d_copies.append(gather_from(3))
 
     def after(p, carry):
         k_own, v_own = sides(pair, p, 0.125)
@@ -355,52 +369,55 @@
         own_v[:, lanes_at(p * 128)] = join_sides(dvs, lo)
         return carry
 
-    def gather(copies, own, d_buf):
-        total = own.astype(F32)
-        for (t, _), copy in zip(peers, copies):
+    e_copies = []
+
+    def send_back(n):
+        total = give[rows_of(head), wide_at(n)].astype(F32)
+        for (t, _), copy in zip(peers, d_copies[n]):
             copy.wait_recv()
-            total = total + d_buf[t].astype(F32)
-        return total
-
-    def send_back(slices, chunk):
+            total = total + d_buf[n, t, :, : total.shape[1]].astype(F32)
         copies = []
         for s, who in earlier:
-            e_send[chunk, s - 1] = jnp.where(tok - owner == s, slices, 0.0).astype(BF16)
-            copies.append(ship(e_send.at[chunk, s - 1], e_recv.at[chunk, s - 1], e_sems, LAG * chunk + s - 1, who))
-        return copies
-
-    ev_copies = send_back(gather(dv_copies, give[rows_of(head), :KV], dv_buf), 1)
+            e_send[n, s - 1] = jnp.where(tok - owner == s, total[:, :PART], 0.0).astype(BF16)
+            copies.append(ship(e_send.at[n, s - 1], e_recv.at[n, s - 1], e_sems, LAG * n + s - 1, who))
+        e_copies.append(copies)
+        return total
+
+    send_back(0)
+    send_back(1)
     lax.fori_loop(0, 1, after, 0)
-    total = gather(dk_copies, give[rows_of(head), KV:], dk_buf)
-    ek_copies = send_back(total[:, :KV], 0)
-    sink_sum = total[:8, KV:] + total[8:, KV:]
+    send_back(2)
+    total = send_back(3)
+    sink_sum = total[:8, PART:] + total[8:, PART:]
     z_send[...] = sink_sum
     z_copies = [(t, ship(z_send, z_recv.at[t], z_sems, t, who)) for t, who in z_peers]
     back_copies.append(ship(near_send.at[:, keys_at], near_back.at[:, keys_at], n_sems, 3, left))
     lax.fori_loop(1, 3, after, 0)
     places = [tail_of(wrap(tok + s, RING), start, parent)[1] for s in range(1, LAG + 1)]
 
-    def land(copies, chunk, at):
-        for copy in copies:
+    f_copies = []
+
+    def land(n):
+        for copy in e_copies[n]:
             copy.wait_recv()
-        arrived = [e_recv[chunk, s].astype(F32) for s in range(LAG)]
+        arrived = [e_recv[n, s].astype(F32) for s in range(LAG)]
 
         def landed(place_):
-            landing = jnp.zeros((ROWS, KV), F32)
+            landing = jnp.zeros((ROWS, PART), F32)
             for s in range(LAG):
                 landing = landing + jnp.where(places[s] == place_, arrived[s], 0.0)
             return landing.astype(BF16)
 
-        copies = []
         for t, who in peers:
-            f_send[chunk, t] = landed(who[1])
-            copies.append(ship(f_send.at[chunk, t], f_recv.at[rows_of(head), at], f_sems, GROUP * chunk + t, who))
-        f_recv[rows_of(head), at] = landed(head)
-        return copies
-
-    f_copies = land(ev_copies, 1, values_at)
+            f_send[n, t] = landed(who[1])
+            f_copies.append(ship(f_send.at[n, t], f_recv.at[rows_of(head), chunk_at(n)], f_sems, GROUP * n + t, who))
+        f_recv[rows_of(head), chunk_at(n)] = landed(head)
+
+    land(0)
+    land(1)
     lax.fori_loop(3, PAIRS, after, 0)
-    f_copies += land(ek_copies, 0, keys_at)
+    land(2)
+    land(3)
     for t, copy in z_copies:
         copy.wait_recv()
         sink_sum = sink_sum + z_recv[t]
@@ -412,8 +429,8 @@
     own_v[...] = own_v[...] + near_back[:, KV:].astype(F32)
     for copy in f_copies:
         copy.wait_recv()
-    key_grad[...] = (own_k[...] + f_recv[:, :KV].astype(F32)).astype(BF16)
-    value_grad[...] = (own_v[...] + f_recv[:, KV:].astype(F32)).astype(BF16)
+    key_grad[...] = (own_k[...] + f_recv[:, KV:].astype(F32)).astype(BF16)
+    value_grad[...] = (own_v[...] + f_recv[:, :KV].astype(F32)).astype(BF16)
     for t, copy in x_copies:
         copy.wait_recv()
         sink_sum = sink_sum + x_recv[t]
@@ -447,9 +464,9 @@
 
 def local(queries, key_states, value_states, out_grad, sink_logits, branch_start, branch_len, parent_list):
     block = pltpu.VMEM((WINDOW, 2 * KV), BF16)
-    slices = pltpu.VMEM((GROUP, ROWS, KV), BF16)
-    slices_more = pltpu.VMEM((GROUP, ROWS, KV + 128), BF16)
-    three = pltpu.VMEM((2, LAG, ROWS, KV), BF16)
+    slices = pltpu.VMEM((GROUP, ROWS, PART), BF16)
+    lags = pltpu.VMEM((LAG, ROWS, PART), BF16)
+    three = pltpu.VMEM((CHUNKS, LAG, ROWS, PART), BF16)
     rows = pltpu.VMEM((WINDOW, 4096), BF16)
     units = (PAIRS, 4, 2 * WINDOW, 256)
     turned = pltpu.VMEM((PAIRS, 4, 128, 256), BF16)
@@ -464,11 +481,11 @@
             pltpu.SMEM((2, 64), jnp.int32), pltpu.SMEM((8,), F32),
             rows, rows,
             pltpu.VMEM((WINDOW, 2 * KV + 128), BF16),
-            slices, slices_more,
+            slices, slices, slices, pltpu.VMEM((GROUP, ROWS, PART + 128), BF16),
             block,
             three,
-            pltpu.VMEM((LAG, ROWS, KV), BF16), pltpu.VMEM((LAG, ROWS, KV), BF16),
-            pltpu.VMEM((2, ROWS, KV), BF16),
+            lags, lags, lags, lags,
+            pltpu.VMEM((CHUNKS, ROWS, PART), BF16),
             block, block,
             pltpu.VMEM((GROUP, 8, 128), F32),
             turned, turned,
@@ -476,17 +493,17 @@
             pltpu.VMEM(units, BF16), pltpu.VMEM(units, BF16),
             pltpu.VMEM((WINDOW, KV), F32), pltpu.VMEM((WINDOW, KV), F32),
             pltpu.VMEM((WINDOW, 2 * KV + 128), BF16),
-            slices, slices_more,
+            pltpu.VMEM((CHUNKS, GROUP, ROWS, PART + 128), BF16),
             block, block,
             three, three,
-            pltpu.VMEM((2, GROUP, ROWS, KV), BF16),
+            pltpu.VMEM((CHUNKS, GROUP, ROWS, PART), BF16),
             block,
             pltpu.VMEM((8, 128), F32), pltpu.VMEM((Z, 8, 128), F32),
             pltpu.VMEM((8, 128), F32), pltpu.VMEM((X, 8, 128), F32),
             pltpu.VMEM((PAIRS, 8, 256), F32), pltpu.VMEM((PAIRS, 8, 256), F32),
             DMA((8,)),
-            DMA((2, 2 * GROUP)), DMA((2, 4)), DMA((2, 2 * LAG)), DMA((2, 2 * GROUP)),
-            DMA((2, 2 * GROUP)), DMA((2, 2 * LAG)), DMA((2, 2 * GROUP)), DMA((2, Z)), DMA((2, X)),
+            DMA((2, CHUNKS * GROUP)), DMA((2, 4)), DMA((2, CHUNKS * LAG)), DMA((2, CHUNKS * GROUP)),
+            DMA((2, CHUNKS * GROUP)), DMA((2, CHUNKS * LAG)), DMA((2, CHUNKS * GROUP)), DMA((2, Z)), DMA((2, X)),
         ],
         compiler_params=pltpu.CompilerParams(
             collective_id=0, has_side_effects=True, vmem_limit_bytes=58 * 1024 * 1024

time: 48 us -> 46.3 us (0.965)
  Pallas kernels: 47.2 us -> 45.6 us
    pallas_call x1, Pallas kernels: 45.8 us -> 44.1 us  [local(): pl.pallas_call(kernel, name='banded', out_shape=tuple((pltpu.VMEM(shape,...]
where the time goes in v5:
time: 46.3 us; the launch traced here: 46.2 us
  Pallas kernels  45.6 us (98%)
  between operations  0.64 us (1%)
    pallas_call x1, Pallas kernels, local(): pl.pallas_call(kernel, name='banded', out_shape=tuple((pltpu.VMEM(shape,...  44.1 us
    pallas_call x1, Pallas kernels, local(): pl.pallas_call(deliver, name='deliver', out_shape=tuple((jax.ShapeDtypeSt...  1.44 us

profile of v5, /device:TPU:1, one launch (start us, length us, event | category | flops | bytes accessed | tf_op | source)
XLA Modules:
  0.0 46.2 jit_solution(11533986768321089075)
XLA Ops:
  0.6 44.1 %banded.1 = (bf16[128,4096]{1,0:T(8,128)(2,1)S(1)}, bf16[128,4096]{1,0:T(8,128)(2,1)S(1)}, bf16[128,512]{1,0:T(8,128)(2,1)S(1)}, bf16[128,512]{1,0:T(8,128)(2,1)S(1)}, f32[8]{0:T(128)S(1)}) custom-call(s32[64]{0:T(128)} %start_in.1, s32[64]{0:T(128)} %length_in.1, s32[2,64]{1,0:T(2,128)} %bitcast.1, f32[8]{0:T(128)} %sink_in.1, bf16[128,4096]{1,0:T(8,128)(2,1)} %queries.1, ...), custom_call_target="tpu_custom_call" | custom-call | tf_op jit(solution)/shard_map/banded/pallas_call | solution.py:473
  44.8 1.4 %deliver.1 = (bf16[128,4096]{1,0:T(8,128)(2,1)}, bf16[128,4096]{1,0:T(8,128)(2,1)}, bf16[128,512]{1,0:T(8,128)(2,1)}, bf16[128,512]{1,0:T(8,128)(2,1)}, f32[8]{0:T(128)}) custom-call(bf16[128,4096]{1,0:T(8,128)(2,1)S(1)} %get-tuple-element.10.refs_0_, bf16[128,4096]{1,0:T(8,128)(2,1)S(1)} %get-tuple-element.11.refs_1_, ...), custom_call_target="tpu_custom_call" | custom-call | tf_op jit(solution)/shard_map/deliver/pallas_call | solution.py:519

commit v6 on v5

--- a/solution.py
+++ b/solution.py
@@ -392,7 +392,7 @@
     z_send[...] = sink_sum
     z_copies = [(t, ship(z_send, z_recv.at[t], z_sems, t, who)) for t, who in z_peers]
     back_copies.append(ship(near_send.at[:, keys_at], near_back.at[:, keys_at], n_sems, 3, left))
-    lax.fori_loop(1, 3, after, 0)
+    lax.fori_loop(1, 2, after, 0)
     places = [tail_of(wrap(tok + s, RING), start, parent)[1] for s in range(1, LAG + 1)]
 
     f_copies = []
@@ -415,7 +415,7 @@
 
     land(0)
     land(1)
-    lax.fori_loop(3, PAIRS, after, 0)
+    lax.fori_loop(2, 3, after, 0)
     land(2)
     land(3)
     for t, copy in z_copies:
@@ -423,6 +423,7 @@
         sink_sum = sink_sum + z_recv[t]
     x_send[...] = sink_sum
     x_copies = [(t, ship(x_send, x_recv.at[t], x_sems, t, who)) for t, who in x_peers]
+    lax.fori_loop(3, 4, after, 0)
     for copy in back_copies:
         copy.wait_recv()
     own_k[...] = own_k[...] + near_back[:, :KV].astype(F32)

time: 46.3 us -> 45.9 us (level)
  no operation moved by 1% of the time
where the time goes in v6:
time: 45.9 us; the launch traced here: 45.8 us
  Pallas kernels  45.2 us (98%)
  between operations  0.64 us (1%)
    pallas_call x1, Pallas kernels, local(): pl.pallas_call(kernel, name='banded', out_shape=tuple((pltpu.VMEM(shape,...  43.8 us
    pallas_call x1, Pallas kernels, local(): pl.pallas_call(deliver, name='deliver', out_shape=tuple((jax.ShapeDtypeSt...  1.44 us

profile of v6, /device:TPU:1, one launch (start us, length us, event | category | flops | bytes accessed | tf_op | source)
XLA Modules:
  0.0 45.8 jit_solution(6697017735189176419)
XLA Ops:
  0.6 43.8 %banded.1 = (bf16[128,4096]{1,0:T(8,128)(2,1)S(1)}, bf16[128,4096]{1,0:T(8,128)(2,1)S(1)}, bf16[128,512]{1,0:T(8,128)(2,1)S(1)}, bf16[128,512]{1,0:T(8,128)(2,1)S(1)}, f32[8]{0:T(128)S(1)}) custom-call(s32[64]{0:T(128)} %start_in.1, s32[64]{0:T(128)} %length_in.1, s32[2,64]{1,0:T(2,128)} %bitcast.1, f32[8]{0:T(128)} %sink_in.1, bf16[128,4096]{1,0:T(8,128)(2,1)} %queries.1, ...), custom_call_target="tpu_custom_call" | custom-call | tf_op jit(solution)/shard_map/banded/pallas_call | solution.py:474
  44.4 1.4 %deliver.1 = (bf16[128,4096]{1,0:T(8,128)(2,1)}, bf16[128,4096]{1,0:T(8,128)(2,1)}, bf16[128,512]{1,0:T(8,128)(2,1)}, bf16[128,512]{1,0:T(8,128)(2,1)}, f32[8]{0:T(128)}) custom-call(bf16[128,4096]{1,0:T(8,128)(2,1)S(1)} %get-tuple-element.10.refs_0_, bf16[128,4096]{1,0:T(8,128)(2,1)S(1)} %get-tuple-element.11.refs_1_, ...), custom_call_target="tpu_custom_call" | custom-call | tf_op jit(solution)/shard_map/deliver/pallas_call | solution.py:520

commit v7 on v6

--- a/solution.py
+++ b/solution.py
@@ -293,7 +293,7 @@
     d_copies = []
     for n in range(2):
         choose(n)
-        lax.fori_loop(2 * n, 2 * n + 2, weigh, 0)
+        lax.fori_loop(2 * n, 2 * n + 2, weigh, 0, unroll=True)
         d_copies.append(gather_from(n))
     back_copies = [ship(near_send.at[:, values_at], near_back.at[:, values_at], n_sems, 2, left)]
 
@@ -324,10 +324,10 @@
         return carry
 
     choose(2)
-    lax.fori_loop(0, 2, incline, 0)
+    lax.fori_loop(0, 2, incline, 0, unroll=True)
     d_copies.append(gather_from(2))
     choose(3)
-    lax.fori_loop(2, PAIRS, incline, 0)
+    lax.fori_loop(2, PAIRS, incline, 0, unroll=True)
     terms = part[...].reshape(GROUP, 4, 256)
     terms = jnp.concatenate([terms[:, :, :128], terms[:, :, 128:]], 1)
     give[:, 2 * KV :] = split_rows(terms).reshape(WINDOW, 128)

time: 45.9 us -> 45.4 us (0.989)
  Pallas kernels: 45.2 us -> 44.7 us
    pallas_call x1, Pallas kernels: 43.8 us -> 43.3 us  [local(): pl.pallas_call(kernel, name='banded', out_shape=tuple((pltpu.VMEM(shape,...]
where the time goes in v7:
time: 45.4 us; the launch traced here: 45.3 us
  Pallas kernels  44.7 us (98%)
  between operations  0.64 us (1%)
    pallas_call x1, Pallas kernels, local(): pl.pallas_call(kernel, name='banded', out_shape=tuple((pltpu.VMEM(shape,...  43.3 us
    pallas_call x1, Pallas kernels, local(): pl.pallas_call(deliver, name='deliver', out_shape=tuple((jax.ShapeDtypeSt...  1.44 us

profile of v7, /device:TPU:1, one launch (start us, length us, event | category | flops | bytes accessed | tf_op | source)
XLA Modules:
  0.0 45.3 jit_solution(2526212910343049841)
XLA Ops:
  0.6 43.3 %banded.1 = (bf16[128,4096]{1,0:T(8,128)(2,1)S(1)}, bf16[128,4096]{1,0:T(8,128)(2,1)S(1)}, bf16[128,512]{1,0:T(8,128)(2,1)S(1)}, bf16[128,512]{1,0:T(8,128)(2,1)S(1)}, f32[8]{0:T(128)S(1)}) custom-call(s32[64]{0:T(128)} %start_in.1, s32[64]{0:T(128)} %length_in.1, s32[2,64]{1,0:T(2,128)} %bitcast.1, f32[8]{0:T(128)} %sink_in.1, bf16[128,4096]{1,0:T(8,128)(2,1)} %queries.1, ...), custom_call_target="tpu_custom_call" | custom-call | tf_op jit(solution)/shard_map/banded/pallas_call | solution.py:474
  43.9 1.4 %deliver.1 = (bf16[128,4096]{1,0:T(8,128)(2,1)}, bf16[128,4096]{1,0:T(8,128)(2,1)}, bf16[128,512]{1,0:T(8,128)(2,1)}, bf16[128,512]{1,0:T(8,128)(2,1)}, f32[8]{0:T(128)}) custom-call(bf16[128,4096]{1,0:T(8,128)(2,1)S(1)} %get-tuple-element.10.refs_0_, bf16[128,4096]{1,0:T(8,128)(2,1)S(1)} %get-tuple-element.11.refs_1_, ...), custom_call_target="tpu_custom_call" | custom-call | tf_op jit(solution)/shard_map/deliver/pallas_call | solution.py:520

commit v8 on v7

--- a/solution.py
+++ b/solution.py
@@ -166,7 +166,10 @@
     place_i = lax.broadcasted_iota(jnp.int32, (WINDOW, 256), 1) & (WINDOW - 1)
     causal = place_j <= place_i
     causal16 = causal.astype(F32).astype(BF16)
-    bias = jnp.where(ok, 0.0, -jnp.inf)
+    causal_both = (lax.broadcasted_iota(jnp.int32, (256, 256), 0) & (WINDOW - 1)) <= (
+        lax.broadcasted_iota(jnp.int32, (256, 256), 1) & (WINDOW - 1)
+    )
+    back_seen = place_j > jnp.where(ok, place_i, WINDOW)
 
     def lanes_at(at, size=128):
         return pl.ds(pl.multiple_of(at, size), size)
@@ -195,7 +198,10 @@
                 ):
                     turned = jnp.concatenate([ref[:, lanes_at(at + 128 * q)].T for q in range(2)], 1)
                     turned_ref[p, 2 * c + half] = turned
-                    own[p, 2 * c + half] = dot(rows, turned, ((1,), (0,)))
+                    product = dot(rows, turned, ((1,), (0,)))
+                    if own is s_own:
+                        product = jnp.where(causal_both, product, -jnp.inf)
+                    own[p, 2 * c + half] = product
         return carry
 
     loads[6].wait()
@@ -273,7 +279,7 @@
                 behind16 = []
                 for e in range(2):
                     at, line = slice(128 * e, 128 * e + 128), 2 * unit + e
-                    scores = jnp.where(causal, s_own[p, unit, at], scores_both[at] + bias)
+                    scores = jnp.where(back_seen, scores_both[at], s_own[p, unit, at])
                     sinks = lines[p, line : line + 1, :]
                     peak = jnp.maximum(jnp.max(scores, axis=0, keepdims=True), sinks)
                     exps = jnp.exp(scores - peak)

time: 45.4 us -> 45.4 us (level)
  no operation moved by 1% of the time
where the time goes in v8:
time: 45.4 us; the launch traced here: 45.3 us
  Pallas kernels  44.6 us (98%)
  between operations  0.64 us (1%)
    pallas_call x1, Pallas kernels, local(): pl.pallas_call(kernel, name='banded', out_shape=tuple((pltpu.VMEM(shape,...  43.2 us
    pallas_call x1, Pallas kernels, local(): pl.pallas_call(deliver, name='deliver', out_shape=tuple((jax.ShapeDtypeSt...  1.44 us

profile of v8, /device:TPU:1, one launch (start us, length us, event | category | flops | bytes accessed | tf_op | source)
XLA Modules:
  0.0 45.3 jit_solution(5535166896572754829)
XLA Ops:
  0.6 43.2 %banded.1 = (bf16[128,4096]{1,0:T(8,128)(2,1)S(1)}, bf16[128,4096]{1,0:T(8,128)(2,1)S(1)}, bf16[128,512]{1,0:T(8,128)(2,1)S(1)}, bf16[128,512]{1,0:T(8,128)(2,1)S(1)}, f32[8]{0:T(128)S(1)}) custom-call(s32[64]{0:T(128)} %start_in.1, s32[64]{0:T(128)} %length_in.1, s32[2,64]{1,0:T(2,128)} %bitcast.1, f32[8]{0:T(128)} %sink_in.1, bf16[128,4096]{1,0:T(8,128)(2,1)} %queries.1, ...), custom_call_target="tpu_custom_call" | custom-call | tf_op jit(solution)/shard_map/banded/pallas_call | solution.py:480
  43.8 1.4 %deliver.1 = (bf16[128,4096]{1,0:T(8,128)(2,1)}, bf16[128,4096]{1,0:T(8,128)(2,1)}, bf16[128,512]{1,0:T(8,128)(2,1)}, bf16[128,512]{1,0:T(8,128)(2,1)}, f32[8]{0:T(128)}) custom-call(bf16[128,4096]{1,0:T(8,128)(2,1)S(1)} %get-tuple-element.10.refs_0_, bf16[128,4096]{1,0:T(8,128)(2,1)S(1)} %get-tuple-element.11.refs_1_, ...), custom_call_target="tpu_custom_call" | custom-call | tf_op jit(solution)/shard_map/deliver/pallas_call | solution.py:526
